TPU v7x, 32 devices: a whole 2x2x4 slice. The times are simulated.
32 devices in a mesh: grp: 4 (over y, core), dev: 8 (over z, x).
Axes of the slice: x: 2, y: 2, z: 4, core: 2. Of those that a mesh axis runs over, the one named last changes fastest.
Arguments:
- pixels: bfloat16 [64, 512, 256], P('grp', 'dev'), may hold values from -16 to 16
- offsets: float32 [64, 512], P('grp', 'dev'), may hold values from -1 to 1
- first_weights: bfloat16 [3, 256, 256], replicated, may hold values from -0.21875 to 0.21875
- second_weights: bfloat16 [3, 256, 256], replicated, may hold values from -0.21875 to 0.21875
- cotangent: bfloat16 [32, 256, 256], P('grp', 'dev'), may hold values from -24 to 24
Outputs:
- grad_pixels: bfloat16 [64, 512, 256], P('grp', 'dev')
- grad_first: float32 [3, 256, 256], replicated
- grad_second: float32 [3, 256, 256], replicated
- level_out: bfloat16 [32, 256, 256], P('grp', 'dev')
All inputs are finite; a program needn't handle non-finite values.
Results may differ from a plain program's by a relative error of at most 0.01.
Values may be sent and summed in bfloat16 or wider, within the bound.
A program may use at most 64 MiB of HBM per device.

v0:
```python
import jax
import jax.numpy as jnp
from jax import lax
from jax.sharding import PartitionSpec as P

NEIGHBOUR_STEPS = (
    (-1, 0, 1.0),
    (1, 0, 1.0),
    (0, -1, 1.0),
    (0, 1, 1.0),
    (-1, -1, 0.5),
    (-1, 1, 0.5),
    (1, -1, 0.5),
    (1, 1, 0.5),
)


def with_halo(block, sides, width):
    for axis, dim in sides:
        count = lax.axis_size(axis)
        forward = [(i, i + 1) for i in range(count - 1)]
        backward = [(target, source) for source, target in forward]
        low = lax.ppermute(
            lax.slice_in_dim(block, block.shape[dim] - width, None, axis=dim), axis, forward
        )
        high = lax.ppermute(lax.slice_in_dim(block, 0, width, axis=dim), axis, backward)
        block = jnp.concatenate([low, block, high], axis=dim)
    return block


def trim(tensor, have_ext, want_ext):
    margin_cut = have_ext - want_ext
    if margin_cut == 0:
        return tensor
    return tensor[
        margin_cut : tensor.shape[0] - margin_cut, margin_cut : tensor.shape[1] - margin_cut
    ]


def graph_parts(offsets, inside, have_ext):
    height = offsets.shape[0] - 2
    breadth = offsets.shape[1] - 2
    centre = offsets[1:-1, 1:-1]
    centre_in = inside[1:-1, 1:-1]
    weights = []
    degree = jnp.zeros(centre.shape, jnp.float32)
    for row_step, col_step, coupling in NEIGHBOUR_STEPS:
        neighbour = offsets[
            1 + row_step : 1 + row_step + height, 1 + col_step : 1 + col_step + breadth
        ]
        present = inside[
            1 + row_step : 1 + row_step + height, 1 + col_step : 1 + col_step + breadth
        ]
        weight = (
            coupling * present * jnp.exp(-(centre - neighbour) * (centre - neighbour)) * centre_in
        )
        weights.append(weight)
        degree = degree + weight
    inverse_root = lax.rsqrt(degree + 1.0 - centre_in) * centre_in
    return (weights, inverse_root, have_ext - 1)


def apply_operator(extended, extent, graph_data):
    weights, inverse_root, have_ext = graph_data
    root_ext = trim(inverse_root, have_ext, extent)
    scaled = root_ext[:, :, None] * extended.astype(jnp.float32)
    height = scaled.shape[0] - 2
    breadth = scaled.shape[1] - 2
    summed = jnp.zeros((height, breadth, scaled.shape[2]), jnp.float32)
    for (row_step, col_step, coupling), weight in zip(NEIGHBOUR_STEPS, weights):
        summed = (
            summed
            + trim(weight, have_ext, extent - 1)[:, :, None]
            * scaled[1 + row_step : 1 + row_step + height, 1 + col_step : 1 + col_step + breadth, :]
        )
    return -root_ext[1:-1, 1:-1, None] * summed


def deep_rim(values):
    return with_halo(values, (("grp", 0), ("dev", 1)), 2)


def forward_terms(values, graph_data):
    first_wide = apply_operator(deep_rim(values), 2, graph_data).astype(jnp.bfloat16)
    second = (2.0 * apply_operator(first_wide, 1, graph_data) - values.astype(jnp.float32)).astype(
        jnp.bfloat16
    )
    first_term = first_wide[1:-1, 1:-1]
    return jnp.concatenate([values, first_term, second], axis=-1)


def project_back(inputs, weights, order_index):
    flattened = inputs.reshape(-1, inputs.shape[-1])
    result = jnp.dot(flattened, weights[order_index].T, preferred_element_type=jnp.float32)
    return result.reshape(inputs.shape[:-1] + (weights.shape[2],))


def backward_terms(cotangent, weights, graph_data):
    widened = deep_rim(cotangent)
    top_term = project_back(widened, weights, 2).astype(jnp.bfloat16)
    middle = (
        project_back(widened[1:-1, 1:-1], weights, 1)
        + 2.0 * apply_operator(top_term, 2, graph_data)
    ).astype(jnp.bfloat16)
    return (
        project_back(cotangent, weights, 0)
        - top_term[2:-2, 2:-2].astype(jnp.float32)
        + apply_operator(middle, 1, graph_data)
    )


def shards(pixels, offsets, first_weights, second_weights, cotangent):
    shard_rows, shard_cols, channels = pixels.shape
    groups = lax.axis_size("grp")
    members = lax.axis_size("dev")
    features = first_weights.shape[0] * channels
    row_ids = lax.axis_index("grp") * shard_rows - 6 + lax.iota(jnp.int32, shard_rows + 12)
    col_ids = lax.axis_index("dev") * shard_cols - 6 + lax.iota(jnp.int32, shard_cols + 12)
    row_in = (row_ids >= 0) & (row_ids < shard_rows * groups)
    col_in = (col_ids >= 0) & (col_ids < shard_cols * members)
    inside = (row_in[:, None] & col_in[None, :]).astype(jnp.float32)
    offset_wide = with_halo(offsets, (("grp", 0), ("dev", 1)), 6)
    fine_graph = graph_parts(offset_wide, inside, 6)
    pooled_offsets = offset_wide.reshape(shard_rows // 2 + 6, 2, shard_cols // 2 + 6, 2).mean(
        axis=(1, 3)
    )
    pooled_graph = graph_parts(pooled_offsets, inside[0::2, 0::2], 3)
    fine_terms = forward_terms(pixels, fine_graph)
    activation = jnp.dot(
        fine_terms.reshape(-1, features),
        first_weights.reshape(features, channels),
        preferred_element_type=jnp.float32,
    ).reshape(shard_rows, shard_cols, channels)
    hidden = jax.nn.silu(activation)
    pooled = (
        hidden.reshape(shard_rows // 2, 2, shard_cols // 2, 2, channels)
        .mean(axis=(1, 3))
        .astype(jnp.bfloat16)
    )
    pooled_terms = forward_terms(pooled, pooled_graph)
    level_out = (
        jnp.dot(
            pooled_terms.reshape(-1, features),
            second_weights.reshape(features, channels),
            preferred_element_type=jnp.float32,
        )
        .astype(jnp.bfloat16)
        .reshape(shard_rows // 2, shard_cols // 2, channels)
    )
    second_sum = jnp.dot(
        pooled_terms.reshape(-1, features).T,
        cotangent.reshape(-1, channels),
        preferred_element_type=jnp.float32,
    ).reshape(second_weights.shape)
    pooled_grad = backward_terms(cotangent, second_weights, pooled_graph)
    spread = jnp.broadcast_to(
        (0.25 * pooled_grad)[:, None, :, None, :],
        (shard_rows // 2, 2, shard_cols // 2, 2, channels),
    ).reshape(shard_rows, shard_cols, channels)
    sigmoid = jax.nn.sigmoid(activation)
    slope_term = sigmoid * (1.0 + activation * (1.0 - sigmoid))
    act_grad = (spread * slope_term).astype(jnp.bfloat16)
    first_sum = jnp.dot(
        fine_terms.reshape(-1, features).T,
        act_grad.reshape(-1, channels),
        preferred_element_type=jnp.float32,
    ).reshape(first_weights.shape)
    grad_pixels = backward_terms(act_grad, first_weights, fine_graph).astype(jnp.bfloat16)
    clip_level = 2.0 * channels
    first_total, second_total = lax.psum((first_sum, second_sum), ("grp", "dev"))
    square_sum = jnp.sum(first_total * first_total) + jnp.sum(second_total * second_total)
    factor = jnp.minimum(1.0, clip_level * lax.rsqrt(square_sum + 1e-06))
    first_out = first_total * factor
    second_out = second_total * factor
    return (grad_pixels, first_out, second_out, level_out)


def solution(mesh):
    return jax.shard_map(
        shards,
        mesh=mesh,
        in_specs=(P("grp", "dev", None), P("grp", "dev"), P(), P(), P("grp", "dev", None)),
        out_specs=(P("grp", "dev", None), P(), P(), P("grp", "dev", None)),
        check_vma=False,
    )
```

profile of v0, /device:TPU:0, one launch (start us, length us, event | category | flops | bytes accessed | tf_op | source)
XLA Modules:
  0.0 247.1 jit_solution(10577706210229969528)
XLA Ops:
  7.2 0.7 fusion.209
  8.0 2.3 collective-permute-start.4
  10.3 1.3 collective-permute-start.5
  11.6 0.8 fusion.206
  12.4 1.3 collective-permute-start.1
  13.7 5.8 %collective-permute-start = (bf16[2,32,256]{2,1,0:T(8,128)(2,1)S(1)}, bf16[2,32,256]{2,1,0:T(8,128)(2,1)S(1)}, u32[]{:S(2)}, u32[]{:S(2)}) collective-permute-start(bf16[2,32,256]{2,1,0:T(8,128)(2,1)S(1)} %get-tuple-element.45), channel_id=1, source_target_pairs={{0,8},{8,16},{16,24},{1,9},{9,17},{17,25},{2,10},{10,18},{18,26},{... | collective-permute-start | bytes 98312 | tf_op jit(solution)/shard_map/ppermute | solution.py:23
  19.5 0.9 fusion.203
  20.4 1.3 collective-permute-start.9
  21.7 0.7 pad_maximum_fusion.5
  22.5 3.4 %collective-permute-start.6 = (f32[28,6]{1,0:T(8,128)S(1)}, f32[28,6]{1,0:T(8,128)S(1)}, u32[]{:S(2)}, u32[]{:S(2)}) collective-permute-start(f32[28,6]{1,0:T(8,128)S(1)} %get-tuple-element.48), channel_id=1, source_target_pairs={{0,1},{1,2},{2,3},{3,4},{4,5},{5,6},{6,7},{8,9},{9,10},{10,11},{11... | collective-permute-start | bytes 2024 | tf_op jit(solution)/shard_map/ppermute | solution.py:23
  25.9 1.3 collective-permute-start.7
  27.3 0.1 slice.561
  27.4 4.0 %collective-permute-start.8 = (bf16[2,64,256]{2,1,0:T(8,128)(2,1)S(1)}, bf16[2,64,256]{2,1,0:T(8,128)(2,1)S(1)}, u32[]{:S(2)}, u32[]{:S(2)}) collective-permute-start(bf16[2,64,256]{2,1,0:T(8,128)(2,1)S(1)} %get-tuple-element.37), channel_id=1, source_target_pairs={{0,8},{8,16},{16,24},{1,9},{9,17},{17,25},{2,10},{10,18},{18,26},{... | collective-permute-start | bytes 196616 | tf_op jit(solution)/shard_map/ppermute | solution.py:23
  31.5 0.8 pad_maximum_fusion.6
  32.5 0.2 reshape.130
  33.3 4.4 %collective-permute-start.2 = (bf16[12,2,256]{2,1,0:T(2,128)(2,1)S(1)}, bf16[12,2,256]{2,1,0:T(2,128)(2,1)S(1)}, u32[]{:S(2)}, u32[]{:S(2)}) collective-permute-start(bf16[12,2,256]{2,1,0:T(2,128)(2,1)S(1)} %get-tuple-element.40), channel_id=1, source_target_pairs={{0,1},{1,2},{2,3},{3,4},{4,5},{5,6},{6,7},{8,9},{9,10},{10,11},{11... | collective-permute-start | bytes 36872 | tf_op jit(solution)/shard_map/ppermute | solution.py:23
  37.7 1.3 collective-permute-start.3
  41.5 2.0 collective-permute-done.3
  43.5 0.3 convert_multiply_fusion.4
  43.8 0.7 fusion.23
  44.6 0.3 copy-done
  45.0 4.8 %collective-permute-start.10 = (bf16[20,2,256]{2,1,0:T(2,128)(2,1)S(1)}, bf16[20,2,256]{2,1,0:T(2,128)(2,1)S(1)}, u32[]{:S(2)}, u32[]{:S(2)}) collective-permute-start(bf16[20,2,256]{2,1,0:T(2,128)(2,1)S(1)} %get-tuple-element.32), channel_id=1, source_target_pairs={{0,1},{1,2},{2,3},{3,4},{4,5},{5,6},{6,7},{8,9},{9,10},{10,11},{11... | collective-permute-start | bytes 61448 | tf_op jit(solution)/shard_map/ppermute | solution.py:23
  49.8 1.3 collective-permute-start.11
  51.2 0.4 fusion.96
  51.6 0.4 broadcast_in_dim.2
  52.0 1.7 reshape.131
  53.7 1.7 collective-permute-done.11
  55.5 0.4 convert_multiply_fusion.1
  56.0 2.3 convert_multiply_fusion.2
  58.2 0.2 slice.819
  58.5 1.6 fusion.38
  60.2 1.7 fusion.45
  61.9 2.0 reshape.135
  64.0 0.7 reduce_sum.38
  64.7 0.6 fusion.205
  65.4 2.0 collective-permute-start.16
  67.4 1.3 collective-permute-start.17
  68.7 0.7 fusion.202
  69.5 5.4 %collective-permute-start.12 = (bf16[2,64,256]{2,1,0:T(8,128)(2,1)}, bf16[2,64,256]{2,1,0:T(8,128)(2,1)}, u32[]{:S(2)}, u32[]{:S(2)}) collective-permute-start(bf16[2,64,256]{2,1,0:T(8,128)(2,1)} %get-tuple-element.34), channel_id=1, source_target_pairs={{0,8},{8,16},{16,24},{1,9},{9,17},{17,25},{2,10},{10,18},{18,26},{... | collective-permute-start | bytes 196616 | tf_op jit(solution)/shard_map/ppermute | solution.py:23
  74.9 1.3 collective-permute-start.13
  76.2 0.8 copy.11
  77.0 0.8 pad_maximum_fusion.9
  77.8 4.4 %collective-permute-start.18 = (bf16[12,2,256]{2,1,0:T(2,128)(2,1)S(1)}, bf16[12,2,256]{2,1,0:T(2,128)(2,1)S(1)}, u32[]{:S(2)}, u32[]{:S(2)}) collective-permute-start(bf16[12,2,256]{2,1,0:T(2,128)(2,1)S(1)} %get-tuple-element.38), channel_id=1, source_target_pairs={{0,1},{1,2},{2,3},{3,4},{4,5},{5,6},{6,7},{8,9},{9,10},{10,11},{11... | collective-permute-start | bytes 36872 | tf_op jit(solution)/shard_map/ppermute | solution.py:23
  82.2 1.3 collective-permute-start.19
  83.6 2.6 %fusion.210 = f32[3,256,256]{2,1,0:T(8,128)} fusion(bf16[3,256,1024]{2,1,0:T(8,128)(2,1)S(1)} %bitcast.61, bf16[1024,256,1]{1,0,2:T(8,128)(2,1)} %bitcast.64), kind=kOutput, calls=%fused_computation.336 | convolution fusion | flops 402653184 | bytes 2883584 | tf_op jit(solution)/shard_map/dot_general | solution.py:163
  86.1 1.6 collective-permute-done.19
  87.8 0.9 convert_multiply_fusion.3
  88.9 0.8 convert_multiply_fusion.5
  89.7 0.4 fusion.86
  90.2 0.2 copy.12
  90.4 0.6 copy-done.7
  91.0 1.1 fusion.211
  92.2 0.8 pad_maximum_fusion.4
  93.0 3.8 %collective-permute-start.14 = (bf16[20,2,256]{2,1,0:T(2,128)(2,1)S(1)}, bf16[20,2,256]{2,1,0:T(2,128)(2,1)S(1)}, u32[]{:S(2)}, u32[]{:S(2)}) collective-permute-start(bf16[20,2,256]{2,1,0:T(2,128)(2,1)S(1)} %get-tuple-element.30), channel_id=1, source_target_pairs={{0,1},{1,2},{2,3},{3,4},{4,5},{5,6},{6,7},{8,9},{9,10},{10,11},{11... | collective-permute-start | bytes 61448 | tf_op jit(solution)/shard_map/ppermute | solution.py:23
  96.8 1.5 collective-permute-start.15
  98.3 0.9 convolution_convert_fusion.2
  99.4 3.1 %collective-permute-done.15 = bf16[20,2,256]{2,1,0:T(2,128)(2,1)S(1)} collective-permute-done((bf16[20,2,256]{2,1,0:T(2,128)(2,1)S(1)}, bf16[20,2,256]{2,1,0:T(2,128)(2,1)S(1)}, u32[]{:S(2)}, u32[]{:S(2)}) %collective-permute-start.15) | collective-permute-done | bytes 20512 | tf_op jit(solution)/shard_map/ppermute | solution.py:26
  102.5 1.3 convert_multiply_fusion
  104.0 3.0 %fusion.2 = f32[18,66,256]{2,1,0:T(8,128)S(1)} fusion(f32[20,68,256]{2,1,0:T(8,128)S(1)} %get-tuple-element.56, bf16[20,2,256]{2,1,0:T(2,128)(2,1)S(1)} %collective-permute-done.15, bf16[20,2,256]{2,1,0:T(2,128)(2,1)S(1)} %collective-permute-done.14, bf16[2,64,256]{2,1,0:T(8,128)(2,1)} %collective-permute-done.13, bf16[16,64,256]{2,1,0:T(8,128)(2,1)S(1)} %copy-done.4, ...), kind=kOutput, calls=%fused_computation.7 | convolution fusion | flops 165141504 | bytes 12783616 | tf_op jit(solution)/shard_map/dot_general | solution.py:94
  107.1 2.6 %fusion.27 = bf16[16,64,256]{2,1,0:T(8,128)(2,1)} fusion(f32[18,66,256]{2,1,0:T(8,128)S(1)} %fusion.2, bf16[20,68,256]{2,1,0:T(8,128)(2,1)S(1)} %get-tuple-element.57, f32[16,64]{1,0:T(8,128)S(1)} %copy-done.67, f32[16,64]{1,0:T(8,128)S(1)} %copy-done.65, f32[16,64]{1,0:T(8,128)S(1)} %copy-done.63, f32[16,64]{1,0:T(8,128)S(1)} %copy-done.61, ...), kind=kOutput, calls=%fused_computation.53 | convolution fusion | flops 139460608 | bytes 10166272 | tf_op jit(solution)/shard_map/dot_general | solution.py:94
  109.7 125.0 %all-reduce.3.cloned.1.call-done = (f32[3,256,256]{2,1,0:T(8,128)}, f32[3,256,256]{2,1,0:T(8,128)}) async-done(((f32[3,256,256]{2,1,0:T(8,128)}, f32[3,256,256]{2,1,0:T(8,128)}), (f32[3,256,256]{2,1,0:T(8,128)}, f32[3,256,256]{2,1,0:T(8,128)})) %all-reduce.3.cloned.1.call-update) | async-done | bytes 1572880 | tf_op jit(solution)/shard_map/psum | solution.py:170
  234.7 2.3 multiply_reduce_fusion
  238.4 0.9 broadcast_multiply_fusion
  239.3 0.9 broadcast_multiply_fusion.1
  (249 shorter events, 4.1 us)
Async XLA Ops:
  7.2 26.1 %copy-start.6 = (bf16[8,32,256]{2,1,0:T(8,128)(2,1)S(1)}, bf16[8,32,256]{2,1,0:T(8,128)(2,1)}, u32[]{:S(2)}) copy-start(bf16[8,32,256]{2,1,0:T(8,128)(2,1)} %param.9) | copy-start | bytes 393220
  7.2 227.6 %all-reduce.3.cloned.1.call-start = ((), (), s32[]{:S(2)}) async-start(), calls=%async_computation | async-start | bytes 3145728 | tf_op jit(solution)/shard_map/psum | solution.py:170
  8.0 13.8 %collective-permute-start.4 = (f32[6,64]{1,0:T(8,128)S(1)}, f32[6,64]{1,0:T(8,128)S(1)}, u32[]{:S(2)}, u32[]{:S(2)}) collective-permute-start(f32[6,64]{1,0:T(8,128)S(1)} %get-tuple-element.52), channel_id=1, source_target_pairs={{0,8},{8,16},{16,24},{1,9},{9,17},{17,25},{2,10},{10,18},{18,26},{... | collective-permute-start | bytes 4616 | tf_op jit(solution)/shard_map/ppermute | solution.py:23
  10.3 11.4 %collective-permute-start.5 = (f32[6,64]{1,0:T(8,128)S(1)}, f32[6,64]{1,0:T(8,128)S(1)}, u32[]{:S(2)}, u32[]{:S(2)}) collective-permute-start(f32[6,64]{1,0:T(8,128)S(1)} %get-tuple-element.53), channel_id=1, source_target_pairs={{8,0},{16,8},{24,16},{9,1},{17,9},{25,17},{10,2},{18,10},{26,18},{... | collective-permute-start | bytes 4616 | tf_op jit(solution)/shard_map/ppermute | solution.py:26
  12.4 20.9 %collective-permute-start.1 = (bf16[2,32,256]{2,1,0:T(8,128)(2,1)S(1)}, bf16[2,32,256]{2,1,0:T(8,128)(2,1)S(1)}, u32[]{:S(2)}, u32[]{:S(2)}) collective-permute-start(bf16[2,32,256]{2,1,0:T(8,128)(2,1)S(1)} %get-tuple-element.44), channel_id=1, source_target_pairs={{8,0},{16,8},{24,16},{9,1},{17,9},{25,17},{10,2},{18,10},{26,18},{... | collective-permute-start | bytes 98312 | tf_op jit(solution)/shard_map/ppermute | solution.py:26
  13.7 19.5 %collective-permute-start = (bf16[2,32,256]{2,1,0:T(8,128)(2,1)S(1)}, bf16[2,32,256]{2,1,0:T(8,128)(2,1)S(1)}, u32[]{:S(2)}, u32[]{:S(2)}) collective-permute-start(bf16[2,32,256]{2,1,0:T(8,128)(2,1)S(1)} %get-tuple-element.45), channel_id=1, source_target_pairs={{0,8},{8,16},{16,24},{1,9},{9,17},{17,25},{2,10},{10,18},{18,26},{... | collective-permute-start | bytes 98312 | tf_op jit(solution)/shard_map/ppermute | solution.py:23
  20.4 24.5 %collective-permute-start.9 = (bf16[2,64,256]{2,1,0:T(8,128)(2,1)S(1)}, bf16[2,64,256]{2,1,0:T(8,128)(2,1)S(1)}, u32[]{:S(2)}, u32[]{:S(2)}) collective-permute-start(bf16[2,64,256]{2,1,0:T(8,128)(2,1)S(1)} %get-tuple-element.36), channel_id=1, source_target_pairs={{8,0},{16,8},{24,16},{9,1},{17,9},{25,17},{10,2},{18,10},{26,18},{... | collective-permute-start | bytes 196616 | tf_op jit(solution)/shard_map/ppermute | solution.py:26
  22.5 4.9 %collective-permute-start.6 = (f32[28,6]{1,0:T(8,128)S(1)}, f32[28,6]{1,0:T(8,128)S(1)}, u32[]{:S(2)}, u32[]{:S(2)}) collective-permute-start(f32[28,6]{1,0:T(8,128)S(1)} %get-tuple-element.48), channel_id=1, source_target_pairs={{0,1},{1,2},{2,3},{3,4},{4,5},{5,6},{6,7},{8,9},{9,10},{10,11},{11... | collective-permute-start | bytes 2024 | tf_op jit(solution)/shard_map/ppermute | solution.py:23
  25.9 5.6 %collective-permute-start.7 = (f32[28,6]{1,0:T(8,128)S(1)}, f32[28,6]{1,0:T(8,128)S(1)}, u32[]{:S(2)}, u32[]{:S(2)}) collective-permute-start(f32[28,6]{1,0:T(8,128)S(1)} %get-tuple-element.49), channel_id=1, source_target_pairs={{1,0},{2,1},{3,2},{4,3},{5,4},{6,5},{7,6},{9,8},{10,9},{11,10},{12... | collective-permute-start | bytes 2024 | tf_op jit(solution)/shard_map/ppermute | solution.py:26
  27.4 17.1 %collective-permute-start.8 = (bf16[2,64,256]{2,1,0:T(8,128)(2,1)S(1)}, bf16[2,64,256]{2,1,0:T(8,128)(2,1)S(1)}, u32[]{:S(2)}, u32[]{:S(2)}) collective-permute-start(bf16[2,64,256]{2,1,0:T(8,128)(2,1)S(1)} %get-tuple-element.37), channel_id=1, source_target_pairs={{0,8},{8,16},{16,24},{1,9},{9,17},{17,25},{2,10},{10,18},{18,26},{... | collective-permute-start | bytes 196616 | tf_op jit(solution)/shard_map/ppermute | solution.py:23
  32.5 11.1 %copy-start.8 = (bf16[3,256,256]{2,1,0:T(8,128)(2,1)S(1)}, bf16[3,256,256]{2,1,0:T(8,128)(2,1)}, u32[]{:S(2)}) copy-start(bf16[3,256,256]{2,1,0:T(8,128)(2,1)} %param.8) | copy-start | bytes 1179652
  32.8 23.1 %copy-start.28 = (f32[18,66]{1,0:T(8,128)}, f32[18,66]{1,0:T(8,128)S(1)}, u32[]{:S(2)}) copy-start(f32[18,66]{1,0:T(8,128)S(1)} %get-tuple-element.46) | copy-start | bytes 14260
  32.8 23.1 %copy-start.30 = (f32[18,66]{1,0:T(8,128)}, f32[18,66]{1,0:T(8,128)S(1)}, u32[]{:S(2)}) copy-start(f32[18,66]{1,0:T(8,128)S(1)} %get-tuple-element.47) | copy-start | bytes 14260
  33.1 11.3 %copy-start.32 = (f32[10,34]{1,0:T(8,128)}, f32[10,34]{1,0:T(8,128)S(1)}, u32[]{:S(2)}) copy-start(f32[10,34]{1,0:T(8,128)S(1)} %get-tuple-element.51) | copy-start | bytes 4084
  33.2 25.2 %copy-start.50 = (f32[16,64]{1,0:T(8,128)}, f32[16,64]{1,0:T(8,128)S(1)}, u32[]{:S(2)}) copy-start(f32[16,64]{1,0:T(8,128)S(1)} %slice_negate_fusion) | copy-start | bytes 12292
  33.3 8.2 %collective-permute-start.2 = (bf16[12,2,256]{2,1,0:T(2,128)(2,1)S(1)}, bf16[12,2,256]{2,1,0:T(2,128)(2,1)S(1)}, u32[]{:S(2)}, u32[]{:S(2)}) collective-permute-start(bf16[12,2,256]{2,1,0:T(2,128)(2,1)S(1)} %get-tuple-element.40), channel_id=1, source_target_pairs={{0,1},{1,2},{2,3},{3,4},{4,5},{5,6},{6,7},{8,9},{9,10},{10,11},{11... | collective-permute-start | bytes 36872 | tf_op jit(solution)/shard_map/ppermute | solution.py:23
  37.7 5.9 %collective-permute-start.3 = (bf16[12,2,256]{2,1,0:T(2,128)(2,1)S(1)}, bf16[12,2,256]{2,1,0:T(2,128)(2,1)S(1)}, u32[]{:S(2)}, u32[]{:S(2)}) collective-permute-start(bf16[12,2,256]{2,1,0:T(2,128)(2,1)S(1)} %get-tuple-element.41), channel_id=1, source_target_pairs={{1,0},{2,1},{3,2},{4,3},{5,4},{6,5},{7,6},{9,8},{10,9},{11,10},{12... | collective-permute-start | bytes 36872 | tf_op jit(solution)/shard_map/ppermute | solution.py:26
  39.0 12.1 %copy-start.68 = (f32[8,32]{1,0:T(8,128)}, f32[8,32]{1,0:T(8,128)S(1)}, u32[]{:S(2)}) copy-start(f32[8,32]{1,0:T(8,128)S(1)} %slice_negate_fusion.1) | copy-start | bytes 3076
  39.1 19.3 %copy-start.52 = (f32[16,64]{1,0:T(8,128)}, f32[16,64]{1,0:T(8,128)S(1)}, u32[]{:S(2)}) copy-start(f32[16,64]{1,0:T(8,128)S(1)} %slice.823) | copy-start | bytes 12292
  39.2 16.7 %copy-start.10 = (f32[18,66]{1,0:T(8,128)}, f32[18,66]{1,0:T(8,128)S(1)}, u32[]{:S(2)}) copy-start(f32[18,66]{1,0:T(8,128)S(1)} %slice.805) | copy-start | bytes 14260
  39.3 19.2 %copy-start.54 = (f32[16,64]{1,0:T(8,128)}, f32[16,64]{1,0:T(8,128)S(1)}, u32[]{:S(2)}) copy-start(f32[16,64]{1,0:T(8,128)S(1)} %slice.821) | copy-start | bytes 12292
  39.3 16.6 %copy-start.12 = (f32[18,66]{1,0:T(8,128)}, f32[18,66]{1,0:T(8,128)S(1)}, u32[]{:S(2)}) copy-start(f32[18,66]{1,0:T(8,128)S(1)} %slice.800) | copy-start | bytes 14260
  39.4 19.0 %copy-start.56 = (f32[16,64]{1,0:T(8,128)}, f32[16,64]{1,0:T(8,128)S(1)}, u32[]{:S(2)}) copy-start(f32[16,64]{1,0:T(8,128)S(1)} %slice.825) | copy-start | bytes 12292
  39.5 16.4 %copy-start.14 = (f32[18,66]{1,0:T(8,128)}, f32[18,66]{1,0:T(8,128)S(1)}, u32[]{:S(2)}) copy-start(f32[18,66]{1,0:T(8,128)S(1)} %slice.807) | copy-start | bytes 14260
  39.6 18.9 %copy-start.58 = (f32[16,64]{1,0:T(8,128)}, f32[16,64]{1,0:T(8,128)S(1)}, u32[]{:S(2)}) copy-start(f32[16,64]{1,0:T(8,128)S(1)} %slice.827) | copy-start | bytes 12292
  39.6 16.3 %copy-start.16 = (f32[18,66]{1,0:T(8,128)}, f32[18,66]{1,0:T(8,128)S(1)}, u32[]{:S(2)}) copy-start(f32[18,66]{1,0:T(8,128)S(1)} %slice.809) | copy-start | bytes 14260
  39.7 18.7 %copy-start.60 = (f32[16,64]{1,0:T(8,128)}, f32[16,64]{1,0:T(8,128)S(1)}, u32[]{:S(2)}) copy-start(f32[16,64]{1,0:T(8,128)S(1)} %slice.829) | copy-start | bytes 12292
  39.8 16.1 %copy-start.18 = (f32[18,66]{1,0:T(8,128)}, f32[18,66]{1,0:T(8,128)S(1)}, u32[]{:S(2)}) copy-start(f32[18,66]{1,0:T(8,128)S(1)} %slice.811) | copy-start | bytes 14260
  39.9 18.6 %copy-start.62 = (f32[16,64]{1,0:T(8,128)}, f32[16,64]{1,0:T(8,128)S(1)}, u32[]{:S(2)}) copy-start(f32[16,64]{1,0:T(8,128)S(1)} %slice.831) | copy-start | bytes 12292
  39.9 16.0 %copy-start.20 = (f32[18,66]{1,0:T(8,128)}, f32[18,66]{1,0:T(8,128)S(1)}, u32[]{:S(2)}) copy-start(f32[18,66]{1,0:T(8,128)S(1)} %slice.813) | copy-start | bytes 14260
  40.0 18.5 %copy-start.64 = (f32[16,64]{1,0:T(8,128)}, f32[16,64]{1,0:T(8,128)S(1)}, u32[]{:S(2)}) copy-start(f32[16,64]{1,0:T(8,128)S(1)} %slice.833) | copy-start | bytes 12292
  40.1 15.9 %copy-start.22 = (f32[18,66]{1,0:T(8,128)}, f32[18,66]{1,0:T(8,128)S(1)}, u32[]{:S(2)}) copy-start(f32[18,66]{1,0:T(8,128)S(1)} %slice.815) | copy-start | bytes 14260
  40.2 18.3 %copy-start.66 = (f32[16,64]{1,0:T(8,128)}, f32[16,64]{1,0:T(8,128)S(1)}, u32[]{:S(2)}) copy-start(f32[16,64]{1,0:T(8,128)S(1)} %slice.835) | copy-start | bytes 12292
  40.3 15.7 %copy-start.24 = (f32[18,66]{1,0:T(8,128)}, f32[18,66]{1,0:T(8,128)S(1)}, u32[]{:S(2)}) copy-start(f32[18,66]{1,0:T(8,128)S(1)} %slice.817) | copy-start | bytes 14260
  40.3 15.1 %copy-start.26 = (f32[20,68]{1,0:T(8,128)}, f32[20,68]{1,0:T(8,128)S(1)}, u32[]{:S(2)}) copy-start(f32[20,68]{1,0:T(8,128)S(1)} %slice.801) | copy-start | bytes 16324
  40.4 10.7 %copy-start.70 = (f32[8,32]{1,0:T(8,128)}, f32[8,32]{1,0:T(8,128)S(1)}, u32[]{:S(2)}) copy-start(f32[8,32]{1,0:T(8,128)S(1)} %slice.767) | copy-start | bytes 3076
  40.6 10.6 %copy-start.72 = (f32[8,32]{1,0:T(8,128)}, f32[8,32]{1,0:T(8,128)S(1)}, u32[]{:S(2)}) copy-start(f32[8,32]{1,0:T(8,128)S(1)} %slice.748) | copy-start | bytes 3076
  40.7 10.4 %copy-start.74 = (f32[8,32]{1,0:T(8,128)}, f32[8,32]{1,0:T(8,128)S(1)}, u32[]{:S(2)}) copy-start(f32[8,32]{1,0:T(8,128)S(1)} %slice.769) | copy-start | bytes 3076
  40.9 10.3 %copy-start.76 = (f32[8,32]{1,0:T(8,128)}, f32[8,32]{1,0:T(8,128)S(1)}, u32[]{:S(2)}) copy-start(f32[8,32]{1,0:T(8,128)S(1)} %slice.771) | copy-start | bytes 3076
  41.0 10.1 %copy-start.78 = (f32[8,32]{1,0:T(8,128)}, f32[8,32]{1,0:T(8,128)S(1)}, u32[]{:S(2)}) copy-start(f32[8,32]{1,0:T(8,128)S(1)} %slice.773) | copy-start | bytes 3076
  41.1 10.0 %copy-start.80 = (f32[8,32]{1,0:T(8,128)}, f32[8,32]{1,0:T(8,128)S(1)}, u32[]{:S(2)}) copy-start(f32[8,32]{1,0:T(8,128)S(1)} %slice.775) | copy-start | bytes 3076
  41.3 9.9 %copy-start.82 = (f32[8,32]{1,0:T(8,128)}, f32[8,32]{1,0:T(8,128)S(1)}, u32[]{:S(2)}) copy-start(f32[8,32]{1,0:T(8,128)S(1)} %slice.777) | copy-start | bytes 3076
  41.4 9.7 %copy-start.84 = (f32[8,32]{1,0:T(8,128)}, f32[8,32]{1,0:T(8,128)S(1)}, u32[]{:S(2)}) copy-start(f32[8,32]{1,0:T(8,128)S(1)} %slice.779) | copy-start | bytes 3076
  45.0 8.8 %collective-permute-start.10 = (bf16[20,2,256]{2,1,0:T(2,128)(2,1)S(1)}, bf16[20,2,256]{2,1,0:T(2,128)(2,1)S(1)}, u32[]{:S(2)}, u32[]{:S(2)}) collective-permute-start(bf16[20,2,256]{2,1,0:T(2,128)(2,1)S(1)} %get-tuple-element.32), channel_id=1, source_target_pairs={{0,1},{1,2},{2,3},{3,4},{4,5},{5,6},{6,7},{8,9},{9,10},{10,11},{11... | collective-permute-start | bytes 61448 | tf_op jit(solution)/shard_map/ppermute | solution.py:23
  49.8 5.7 %collective-permute-start.11 = (bf16[20,2,256]{2,1,0:T(2,128)(2,1)S(1)}, bf16[20,2,256]{2,1,0:T(2,128)(2,1)S(1)}, u32[]{:S(2)}, u32[]{:S(2)}) collective-permute-start(bf16[20,2,256]{2,1,0:T(2,128)(2,1)S(1)} %get-tuple-element.33), channel_id=1, source_target_pairs={{1,0},{2,1},{3,2},{4,3},{5,4},{6,5},{7,6},{9,8},{10,9},{11,10},{12... | collective-permute-start | bytes 61448 | tf_op jit(solution)/shard_map/ppermute | solution.py:26
  61.9 6.8 %copy-start.3 = (bf16[16,64,256]{2,1,0:T(8,128)(2,1)}, bf16[16,64,256]{2,1,0:T(8,128)(2,1)S(1)}, u32[]{:S(2)}) copy-start(bf16[16,64,256]{2,1,0:T(8,128)(2,1)S(1)} %get-tuple-element.29) | copy-start | bytes 1572868
  65.4 11.6 %collective-permute-start.16 = (bf16[2,32,256]{2,1,0:T(8,128)(2,1)}, bf16[2,32,256]{2,1,0:T(8,128)(2,1)}, u32[]{:S(2)}, u32[]{:S(2)}) collective-permute-start(bf16[2,32,256]{2,1,0:T(8,128)(2,1)} %get-tuple-element.42), channel_id=1, source_target_pairs={{0,8},{8,16},{16,24},{1,9},{9,17},{17,25},{2,10},{10,18},{18,26},{... | collective-permute-start | bytes 98312 | tf_op jit(solution)/shard_map/ppermute | solution.py:23
  67.4 9.6 %collective-permute-start.17 = (bf16[2,32,256]{2,1,0:T(8,128)(2,1)}, bf16[2,32,256]{2,1,0:T(8,128)(2,1)}, u32[]{:S(2)}, u32[]{:S(2)}) collective-permute-start(bf16[2,32,256]{2,1,0:T(8,128)(2,1)} %get-tuple-element.43), channel_id=1, source_target_pairs={{8,0},{16,8},{24,16},{9,1},{17,9},{25,17},{10,2},{18,10},{26,18},{... | collective-permute-start | bytes 98312 | tf_op jit(solution)/shard_map/ppermute | solution.py:26
  69.5 22.7 %collective-permute-start.12 = (bf16[2,64,256]{2,1,0:T(8,128)(2,1)}, bf16[2,64,256]{2,1,0:T(8,128)(2,1)}, u32[]{:S(2)}, u32[]{:S(2)}) collective-permute-start(bf16[2,64,256]{2,1,0:T(8,128)(2,1)} %get-tuple-element.34), channel_id=1, source_target_pairs={{0,8},{8,16},{16,24},{1,9},{9,17},{17,25},{2,10},{10,18},{18,26},{... | collective-permute-start | bytes 196616 | tf_op jit(solution)/shard_map/ppermute | solution.py:23
  74.9 17.2 %collective-permute-start.13 = (bf16[2,64,256]{2,1,0:T(8,128)(2,1)}, bf16[2,64,256]{2,1,0:T(8,128)(2,1)}, u32[]{:S(2)}, u32[]{:S(2)}) collective-permute-start(bf16[2,64,256]{2,1,0:T(8,128)(2,1)} %get-tuple-element.35), channel_id=1, source_target_pairs={{8,0},{16,8},{24,16},{9,1},{17,9},{25,17},{10,2},{18,10},{26,18},{... | collective-permute-start | bytes 196616 | tf_op jit(solution)/shard_map/ppermute | solution.py:26
  77.8 8.3 %collective-permute-start.18 = (bf16[12,2,256]{2,1,0:T(2,128)(2,1)S(1)}, bf16[12,2,256]{2,1,0:T(2,128)(2,1)S(1)}, u32[]{:S(2)}, u32[]{:S(2)}) collective-permute-start(bf16[12,2,256]{2,1,0:T(2,128)(2,1)S(1)} %get-tuple-element.38), channel_id=1, source_target_pairs={{0,1},{1,2},{2,3},{3,4},{4,5},{5,6},{6,7},{8,9},{9,10},{10,11},{11... | collective-permute-start | bytes 36872 | tf_op jit(solution)/shard_map/ppermute | solution.py:23
  82.2 5.6 %collective-permute-start.19 = (bf16[12,2,256]{2,1,0:T(2,128)(2,1)S(1)}, bf16[12,2,256]{2,1,0:T(2,128)(2,1)S(1)}, u32[]{:S(2)}, u32[]{:S(2)}) collective-permute-start(bf16[12,2,256]{2,1,0:T(2,128)(2,1)S(1)} %get-tuple-element.39), channel_id=1, source_target_pairs={{1,0},{2,1},{3,2},{4,3},{5,4},{6,5},{7,6},{9,8},{10,9},{11,10},{12... | collective-permute-start | bytes 36872 | tf_op jit(solution)/shard_map/ppermute | solution.py:26
  83.5 5.2 %copy-start.33 = (f32[10,34]{1,0:T(8,128)S(1)}, f32[10,34]{1,0:T(8,128)}, u32[]{:S(2)}) copy-start(f32[10,34]{1,0:T(8,128)} %copy-done.32) | copy-start | bytes 4084
  83.5 5.2 %copy-start.35 = (f32[10,34]{1,0:T(8,128)S(1)}, f32[10,34]{1,0:T(8,128)}, u32[]{:S(2)}) copy-start(f32[10,34]{1,0:T(8,128)} %copy-done.34) | copy-start | bytes 4084
  83.5 5.2 %copy-start.37 = (f32[10,34]{1,0:T(8,128)S(1)}, f32[10,34]{1,0:T(8,128)}, u32[]{:S(2)}) copy-start(f32[10,34]{1,0:T(8,128)} %copy-done.36) | copy-start | bytes 4084
  83.5 5.2 %copy-start.39 = (f32[10,34]{1,0:T(8,128)S(1)}, f32[10,34]{1,0:T(8,128)}, u32[]{:S(2)}) copy-start(f32[10,34]{1,0:T(8,128)} %copy-done.38) | copy-start | bytes 4084
  83.5 5.2 %copy-start.41 = (f32[10,34]{1,0:T(8,128)S(1)}, f32[10,34]{1,0:T(8,128)}, u32[]{:S(2)}) copy-start(f32[10,34]{1,0:T(8,128)} %copy-done.40) | copy-start | bytes 4084
  83.5 5.2 %copy-start.43 = (f32[10,34]{1,0:T(8,128)S(1)}, f32[10,34]{1,0:T(8,128)}, u32[]{:S(2)}) copy-start(f32[10,34]{1,0:T(8,128)} %copy-done.42) | copy-start | bytes 4084
  83.5 5.2 %copy-start.45 = (f32[10,34]{1,0:T(8,128)S(1)}, f32[10,34]{1,0:T(8,128)}, u32[]{:S(2)}) copy-start(f32[10,34]{1,0:T(8,128)} %copy-done.44) | copy-start | bytes 4084
  90.2 8.1 %copy-start.9 = (bf16[3,256,256]{2,1,0:T(8,128)(2,1)S(1)}, bf16[3,256,256]{2,1,0:T(8,128)(2,1)}, u32[]{:S(2)}) copy-start(bf16[3,256,256]{2,1,0:T(8,128)(2,1)} %param.8) | copy-start | bytes 1179652
  93.0 9.6 %copy-start.27 = (f32[20,68]{1,0:T(8,128)S(1)}, f32[20,68]{1,0:T(8,128)}, u32[]{:S(2)}) copy-start(f32[20,68]{1,0:T(8,128)} %copy-done.26) | copy-start | bytes 16324
  93.0 9.6 %copy-start.87 = (bf16[3,256,256]{2,1,0:T(8,128)(2,1)S(1)}, bf16[3,256,256]{2,1,0:T(8,128)(2,1)}, u32[]{:S(2)}) copy-start(bf16[3,256,256]{2,1,0:T(8,128)(2,1)} %param.7) | copy-start | bytes 1179652
  93.0 6.4 %collective-permute-start.14 = (bf16[20,2,256]{2,1,0:T(2,128)(2,1)S(1)}, bf16[20,2,256]{2,1,0:T(2,128)(2,1)S(1)}, u32[]{:S(2)}, u32[]{:S(2)}) collective-permute-start(bf16[20,2,256]{2,1,0:T(2,128)(2,1)S(1)} %get-tuple-element.30), channel_id=1, source_target_pairs={{0,1},{1,2},{2,3},{3,4},{4,5},{5,6},{6,7},{8,9},{9,10},{10,11},{11... | collective-permute-start | bytes 61448 | tf_op jit(solution)/shard_map/ppermute | solution.py:23
  96.8 5.7 %collective-permute-start.15 = (bf16[20,2,256]{2,1,0:T(2,128)(2,1)S(1)}, bf16[20,2,256]{2,1,0:T(2,128)(2,1)S(1)}, u32[]{:S(2)}, u32[]{:S(2)}) collective-permute-start(bf16[20,2,256]{2,1,0:T(2,128)(2,1)S(1)} %get-tuple-element.31), channel_id=1, source_target_pairs={{1,0},{2,1},{3,2},{4,3},{5,4},{6,5},{7,6},{9,8},{10,9},{11,10},{12... | collective-permute-start | bytes 61448 | tf_op jit(solution)/shard_map/ppermute | solution.py:26
  (45 other events, 134.9 us)
Sparse Core Ops, SparseCore 0:
  99.4 135.2 all-reduce.2
where the time goes:
time: 248 us; the launch traced here: 247 us
  waiting for transfers between devices  134 us (54%)
  starting transfers between devices  53.5 us (22%)
  between operations  16.9 us (7%)
  other arithmetic  15.3 us (6%)
  matrix products  14.6 us (6%)
  local copies, waits for them, and re-layouts  13.2 us (5%)
    psum x1, waiting for transfers between devices, shards(): lax.psum((first_sum, second_sum), ('grp', 'dev'))  125 us
    ppermute x10, starting transfers between devices, with_halo(): lax.ppermute(lax.slice_in_dim(block, block.shape[dim] - width, None, axis...  40.4 us
    ppermute x10, starting transfers between devices, with_halo(): lax.ppermute(lax.slice_in_dim(block, 0, width, axis=dim), axis, backward)  13.1 us
    ppermute x10, waiting for transfers between devices, with_halo(): lax.ppermute(lax.slice_in_dim(block, 0, width, axis=dim), axis, backward)  8.61 us
    dot_general x6, matrix products, project_back(): jnp.dot(flattened, weights[order_index].T, preferred_element_type=jnp.flo...  8.25 us
  transfers between devices with their start and end apart: 21, of which 6 were waited for; matrix products, arithmetic and copies ran while one was open for 11% of the time, Pallas kernels for 0%

commit v1 on v0

v1 whole, which is shorter than its diff:
```python
import functools

import jax
import jax.numpy as jnp
from jax import lax
from jax.experimental import pallas as pl
from jax.experimental.pallas import tpu as pltpu
from jax.sharding import PartitionSpec as P

MESH = pl.DeviceIdType.MESH
F32 = jnp.float32
BF16 = jnp.bfloat16
STEPS = (
    (-1, 0, 1.0),
    (1, 0, 1.0),
    (0, -1, 1.0),
    (0, 1, 1.0),
    (-1, -1, 0.5),
    (-1, 1, 0.5),
    (1, -1, 0.5),
    (1, 1, 0.5),
)
INDEX = {(dr, dc): k for k, (dr, dc, _) in enumerate(STEPS)}
LANES = 128
RIM = 8
FINE_UP = 6
POOL_UP = 4


def edge_coefficients(offsets, inside):
    rows = offsets.shape[0]

    def moved(x, dr, dc):
        if dr:
            x = pltpu.roll(x, (-dr) % rows, 0)
        if dc:
            x = pltpu.roll(x, (-dc) % LANES, 1)
        return x

    weights = []
    degree = jnp.zeros_like(offsets)
    for dr, dc, coupling in STEPS:
        gap = offsets - moved(offsets, dr, dc)
        weight = coupling * inside * moved(inside, dr, dc) * jnp.exp(-gap * gap)
        weights.append(weight)
        degree = degree + weight
    root = lax.rsqrt(jnp.maximum(degree, 1e-30)) * inside
    found = []
    for (dr, dc, _), weight in zip(STEPS, weights):
        value = -root * weight * moved(root, dr, dc)
        if dc:
            value = pltpu.roll(value, dc % LANES, 1)
        found.append(value)
    return found


def spread_coefficients(found, stack, turned, coefs, shift, first, last):
    rows = found[0].shape[0]
    for k, value in enumerate(found):
        stack[pl.ds(k * rows, rows), :] = value
    for b in range(stack.shape[0] // LANES):
        turned[b] = stack[pl.ds(b * LANES, LANES), :].T
    width = coefs.shape[2]
    for k in range(len(STEPS)):
        for e in range(first, last):
            block, lane = divmod(k * rows + e + shift, LANES)
            coefs[k, e] = jnp.broadcast_to(
                turned[block, pl.ds(0, width), pl.ds(lane, 1)], (width, LANES)
            )


def stencil(values, coefs, row, coef_row, half):
    lanes = pl.ds(half * LANES, LANES)
    around = [values[row + dr, :, lanes] for dr in (-1, 0, 1)]
    width = around[0].shape[0]

    def column(dc):
        total = None
        for dr in (-1, 0, 1):
            if (dr, dc) in INDEX:
                term = coefs[INDEX[dr, dc], coef_row] * around[dr + 1]
                total = term if total is None else total + term
        return total

    return pltpu.roll(column(-1), 1, 0) + column(0) + pltpu.roll(column(1), width - 1, 0)


def dot(a, b):
    return lax.dot_general(a, b, (((1,), (0,)), ((), ())), preferred_element_type=F32)


def dot_rows(a, b):
    return lax.dot_general(a, b, (((1,), (1,)), ((), ())), preferred_element_type=F32)


def dot_sum(a, b):
    return lax.dot_general(a, b, (((0,), (0,)), ((), ())), preferred_element_type=F32)


def split_dot(matrix, value):
    high = value.astype(BF16)
    low = (value - high.astype(F32)).astype(BF16)
    return dot(matrix, high) + dot(matrix, low)


def kernel(
    groups, members, chunk,
    px, off, w1, w2, cot,
    gp, gfirst, gsecond, level,
    off_own, off_in,
    px_pack, px_v, px_h, px_c,
    ct_pack, ct_v, ct_h, ct_c,
    off_ext, stack, turned, pstack, pturned, coefs, pcoefs,
    t0, t1, t2, v0, v1, slope,
    c0, cm, q0, q1, q2, z0, z1, ptop, pone, pzero, pmid, pgrad,
    ag, agm, mid,
    sums, sb, full, in_a, in_b, in_c,
    halo_send, halo_recv, sum_send, sum_recv,
):
    rows, cols, feats = px.shape
    prows, pcols = cot.shape[:2]
    width, pwidth = cols + 2 * RIM, pcols + 2 * RIM
    halves = feats // LANES
    g, d = lax.axis_index("grp"), lax.axis_index("dev")

    around = []
    for dr, dc, _ in STEPS:
        ng, nd = g + dr, d + dc
        exists = (ng >= 0) & (ng < groups) & (nd >= 0) & (nd < members)
        around.append((dr, dc, exists, (ng, nd)))
    core, quad, line = lax.rem(g, 2), (g // 2) * 2 + lax.rem(d, 2), d // 2
    lines = members // 2
    peer_a = (g + 1 - 2 * core, d)
    peers_b, peers_c = [], []
    for j in range(1, groups):
        q = lax.rem(quad + j, groups)
        peers_b.append((q, ((q // 2) * 2 + core, line * 2 + lax.rem(q, 2))))
    for j in range(1, lines):
        z = lax.rem(line + j, lines)
        peers_c.append((z, (g, z * 2 + lax.rem(d, 2))))

    barrier = pltpu.get_barrier_semaphore()
    for dr, dc, exists, peer in around:
        @pl.when(exists)
        def _():
            pl.semaphore_signal(barrier, inc=1, device_id=peer, device_id_type=MESH)
    for peer in [peer_a] + [p for _, p in peers_b] + [p for _, p in peers_c]:
        pl.semaphore_signal(barrier, inc=1, device_id=peer, device_id_type=MESH)

    off_own[...] = jnp.zeros_like(off_own)
    off_own[:, pl.ds(0, cols)] = off[...]
    for source, pack in ((px, px_pack), (cot, ct_pack)):
        edge = source.shape[1]

        def pack_pair(i, _):
            for side, start in ((0, 0), (1, edge - 16)):
                cut = 0 if side == 0 else 8
                parts = [
                    source[2 * i + s, pl.ds(start, 16), :].astype(F32)[cut : cut + 8]
                    for s in (0, 1)
                ]
                pack[side, i] = jnp.concatenate(parts, axis=0).astype(BF16)
            return 0

        lax.fori_loop(0, source.shape[0] // 2, pack_pair, 0)

    greeted = groups + lines - 1
    for dr, dc, exists, peer in around:
        greeted = greeted + jnp.where(exists, 1, 0)
    pl.semaphore_wait(barrier, greeted)

    def halo_copies(dr, dc, peer):
        k, o = INDEX[dr, dc], INDEX[-dr, -dc]
        made = []
        for a, (src, pack, up, v, h, c) in enumerate(
            ((px, px_pack, FINE_UP, px_v, px_h, px_c), (cot, ct_pack, POOL_UP, ct_v, ct_h, ct_c))
        ):
            n = src.shape[0]
            if dc == 0:
                source = src.at[pl.ds(0 if dr < 0 else n - up, up)]
                land, here = v.at[o], v.at[k]
            elif dr == 0:
                source = pack.at[0 if dc < 0 else 1]
                land, here = h.at[o - 2], h.at[k - 2]
            else:
                tiles = up // 2
                source = pack.at[
                    0 if dc < 0 else 1, pl.ds(0 if dr < 0 else n // 2 - tiles, tiles)
                ]
                land, here = c.at[o - 4], c.at[k - 4]
            made.append((a, source, land, here))
        made.append((2, off_own, off_in.at[o], off_in.at[k]))
        outgoing, incoming = [], []
        for a, source, land, here in made:
            copy = functools.partial(
                pltpu.make_async_remote_copy, src_ref=source, send_sem=halo_send.at[a, k],
                device_id=peer, device_id_type=MESH,
            )
            outgoing.append(
                functools.partial(copy, dst_ref=land, recv_sem=halo_recv.at[a, o])
            )
            incoming.append(
                (here, functools.partial(copy, dst_ref=here, recv_sem=halo_recv.at[a, k]))
            )
        return outgoing, incoming

    for dr, dc, exists, peer in around:
        @pl.when(exists)
        def _():
            for copy in reversed(halo_copies(dr, dc, peer)[0]):
                copy().start()

        @pl.when(jnp.logical_not(exists))
        def _():
            for here, _ in halo_copies(dr, dc, peer)[1]:
                here[...] = jnp.zeros(here.shape, here.dtype)

    for dr, dc, exists, peer in around:
        @pl.when(exists)
        def _():
            halo_copies(dr, dc, peer)[1][2][1]().wait_recv()

    def lay(left, own, right):
        lane = lax.broadcasted_iota(jnp.int32, own.shape, 1)
        out = jnp.where(lane < RIM, pltpu.roll(left, (RIM - cols) % LANES, 1), 0.0)
        out = jnp.where((lane >= RIM) & (lane < cols + RIM), pltpu.roll(own, RIM, 1), out)
        return jnp.where(
            (lane >= cols + RIM) & (lane < width), pltpu.roll(right, cols + RIM, 1), out
        )

    def slot(dr, dc, cut):
        return off_in[INDEX[dr, dc], cut, :]

    high, low = pl.ds(rows - 8, 8), pl.ds(0, 8)
    off_ext[pl.ds(0, 8), :] = lay(slot(-1, -1, high), slot(-1, 0, high), slot(-1, 1, high))
    off_ext[pl.ds(8, rows), :] = lay(off_in[INDEX[0, -1]], off_own[...], off_in[INDEX[0, 1]])
    off_ext[pl.ds(8 + rows, 8), :] = lay(slot(1, -1, low), slot(1, 0, low), slot(1, 1, low))

    def within(shape, row_start, col_start, row_end, col_end, used):
        r = lax.broadcasted_iota(jnp.int32, shape, 0) + row_start
        lane = lax.broadcasted_iota(jnp.int32, shape, 1)
        c = lane + col_start
        ok = (r >= 0) & (r < row_end) & (c >= 0) & (c < col_end) & (lane < used)
        return jnp.where(ok, 1.0, 0.0).astype(F32)

    offsets = off_ext[...]
    inside = within(
        offsets.shape, g * rows - 8, d * cols - RIM, groups * rows, members * cols, width
    )
    spread_coefficients(
        edge_coefficients(offsets, inside), stack, turned, coefs, 2, 1, rows + 2 * FINE_UP - 1
    )
    pshape = (prows + 2 * POOL_UP, LANES)
    a_r = lax.broadcasted_iota(jnp.int32, (pshape[0], rows + 16), 0)
    a_f = lax.broadcasted_iota(jnp.int32, (pshape[0], rows + 16), 1)
    by_row = jnp.where((a_f == 2 * a_r) | (a_f == 2 * a_r + 1), 0.5, 0.0).astype(F32)
    b_f = lax.broadcasted_iota(jnp.int32, (LANES, LANES), 0)
    b_l = lax.broadcasted_iota(jnp.int32, (LANES, LANES), 1)
    by_col = jnp.where((b_f == 2 * b_l - 8) | (b_f == 2 * b_l - 7), 0.5, 0.0).astype(F32)
    exact = functools.partial(
        jnp.dot, precision=lax.Precision.HIGHEST, preferred_element_type=F32
    )
    poffsets = exact(exact(by_row, offsets), by_col)
    pinside = within(
        pshape, g * prows - POOL_UP, d * pcols - RIM, groups * prows, members * pcols, pwidth
    )
    spread_coefficients(
        edge_coefficients(poffsets, pinside), pstack, pturned, pcoefs, 0, 1,
        prows + 2 * POOL_UP - 1,
    )

    for dr, dc, exists, peer in around:
        @pl.when(exists)
        def _():
            outgoing, incoming = halo_copies(dr, dc, peer)
            for _, copy in incoming[:2]:
                copy().wait_recv()
            for copy in outgoing:
                copy().wait_send()

    def assemble(store, start, pairs, middle, left, right):
        def pair(i, _):
            lt, rt = left(i).astype(F32), right(i).astype(F32)
            for s in (0, 1):
                row = jnp.concatenate(
                    [
                        lt[8 * s : 8 * s + 8],
                        middle(2 * i + s).astype(F32),
                        rt[8 * s : 8 * s + 8],
                    ],
                    axis=0,
                )
                store(start + 2 * i + s, row)
            return 0

        lax.fori_loop(0, pairs, pair, 0)

    def store_px(e, row):
        v0[e] = row
        t0[e] = row.astype(BF16)

    def store_cot(e, row):
        c0[e] = row.astype(BF16)

    for store, src, up, v, h, c in (
        (store_px, px, FINE_UP, px_v, px_h, px_c),
        (store_cot, cot, POOL_UP, ct_v, ct_h, ct_c),
    ):
        n = src.shape[0]
        assemble(store, 0, up // 2, lambda r: v[0, r], lambda i: c[0, i], lambda i: c[1, i])
        assemble(store, up, n // 2, lambda r: src[r], lambda i: h[0, i], lambda i: h[1, i])
        assemble(store, up + n, up // 2, lambda r: v[1, r], lambda i: c[2, i], lambda i: c[3, i])

    def fine_one(e, _):
        for half in range(halves):
            value = stencil(v0, coefs, e, e, half).astype(BF16)
            t1[e, :, pl.ds(half * LANES, LANES)] = value
            v1[e, :, pl.ds(half * LANES, LANES)] = value.astype(F32)
        return 0

    def fine_two(e, _):
        for half in range(halves):
            lanes = pl.ds(half * LANES, LANES)
            t2[e, :, lanes] = (
                2.0 * stencil(v1, coefs, e, e, half) - v0[e, :, lanes]
            ).astype(BF16)
        return 0

    lax.fori_loop(1, rows + 2 * FINE_UP - 1, fine_one, 0)
    lax.fori_loop(2, rows + 2 * FINE_UP - 2, fine_two, 0)

    def pool_matrix(shape, fine_dim):
        f = lax.broadcasted_iota(jnp.int32, shape, fine_dim)
        p = lax.broadcasted_iota(jnp.int32, shape, 1 - fine_dim)
        return jnp.where((f == 2 * p - 8) | (f == 2 * p - 7), 0.25, 0.0).astype(BF16)

    gather_pool = pool_matrix((pwidth, width), 1)
    spread_pool = pool_matrix((width, pwidth), 0)

    def activate(i, _):
        e = 2 + 4 * i
        flat = (4 * width, feats)
        a = dot(t0[pl.ds(e, 4)].reshape(flat), w1[0])
        a = a + dot(t1[pl.ds(e, 4)].reshape(flat), w1[1])
        a = a + dot(t2[pl.ds(e, 4)].reshape(flat), w1[2])
        s = jax.nn.sigmoid(a)
        slope[pl.ds(4 * i, 4)] = (s * (1.0 + a * (1.0 - s))).reshape(4, width, feats)
        hidden = a * s
        for p in (0, 1):
            both = (
                hidden[2 * p * width : (2 * p + 1) * width]
                + hidden[(2 * p + 1) * width : (2 * p + 2) * width]
            )
            value = split_dot(gather_pool, both).astype(BF16)
            q0[2 + 2 * i + p] = value
            z0[2 + 2 * i + p] = value.astype(F32)
        return 0

    lax.fori_loop(0, (prows + 4) // 2, activate, 0)

    def project_pool(i, _):
        x = c0[pl.ds(4 * i, 4)].reshape(4 * pwidth, feats)
        wide = (4, pwidth, feats)
        ptop[pl.ds(4 * i, 4)] = dot_rows(x, w2[2]).astype(BF16).astype(F32).reshape(wide)
        pone[pl.ds(4 * i, 4)] = dot_rows(x, w2[1]).reshape(wide)
        pzero[pl.ds(4 * i, 4)] = dot_rows(x, w2[0]).reshape(wide)
        return 0

    lax.fori_loop(0, (prows + 2 * POOL_UP) // 4, project_pool, 0)

    def pool_middle(e, _):
        for half in range(halves):
            lanes = pl.ds(half * LANES, LANES)
            pmid[e, :, lanes] = (
                (pone[e, :, lanes] + 2.0 * stencil(ptop, pcoefs, e, e, half))
                .astype(BF16)
                .astype(F32)
            )
        return 0

    def pool_grad(e, _):
        for half in range(halves):
            lanes = pl.ds(half * LANES, LANES)
            pgrad[e, :, lanes] = (
                pzero[e, :, lanes] - ptop[e, :, lanes] + stencil(pmid, pcoefs, e, e, half)
            )
        return 0

    lax.fori_loop(2, prows + 2 * POOL_UP - 2, pool_middle, 0)
    lax.fori_loop(3, prows + 2 * POOL_UP - 3, pool_grad, 0)

    col = lax.broadcasted_iota(jnp.int32, (width, feats), 0)
    own_cols = (col >= RIM) & (col < cols + RIM)

    def act_grad(i, _):
        wide = split_dot(spread_pool, pgrad[i + 3])
        for s in (0, 1):
            value = wide * slope[2 * i + 2 + s]
            ag[2 * i + s] = value.astype(BF16)
            agm[2 * i + s] = jnp.where(own_cols, value, 0.0).astype(BF16)
        return 0

    lax.fori_loop(0, prows + 2, act_grad, 0)

    def pool_one(e, _):
        for half in range(halves):
            lanes = pl.ds(half * LANES, LANES)
            value = stencil(z0, pcoefs, e, e, half).astype(BF16)
            q1[e, :, lanes] = value
            z1[e, :, lanes] = value.astype(F32)
        return 0

    def pool_two(e, _):
        for half in range(halves):
            lanes = pl.ds(half * LANES, LANES)
            q2[e, :, lanes] = (
                2.0 * stencil(z1, pcoefs, e, e, half) - z0[e, :, lanes]
            ).astype(BF16)
        return 0

    lax.fori_loop(POOL_UP - 1, prows + POOL_UP + 1, pool_one, 0)
    lax.fori_loop(POOL_UP, prows + POOL_UP, pool_two, 0)

    pcol = lax.broadcasted_iota(jnp.int32, (pwidth, feats), 0)
    own_pcols = (pcol >= RIM) & (pcol < pcols + RIM)

    def mask_cot(r, _):
        cm[r] = jnp.where(own_pcols, c0[POOL_UP + r].astype(F32), 0.0).astype(BF16)
        return 0

    lax.fori_loop(0, prows, mask_cot, 0)

    if sums.shape[0] > 6 * feats:
        sums[pl.ds(6 * feats, sums.shape[0] - 6 * feats), :] = jnp.zeros(
            (sums.shape[0] - 6 * feats, feats), F32
        )
    back = agm[pl.ds(2, rows)].reshape(rows * width, feats)
    for k, term in enumerate((t0, t1, t2)):
        x = term[pl.ds(FINE_UP, rows)].reshape(rows * width, feats)
        sums[pl.ds(k * feats, feats), :] = dot_sum(x, back)
    pback = cm[...].reshape(prows * pwidth, feats)
    for k, term in enumerate((q0, q1, q2)):
        x = term[pl.ds(POOL_UP, prows)].reshape(prows * pwidth, feats)
        sums[pl.ds((3 + k) * feats, feats), :] = dot_sum(x, pback)

    total = sums.shape[0]
    half_rows = total // 2
    block_rows = half_rows // groups

    def at(start, size):
        return pl.ds(pl.multiple_of(start, 16), size)

    def send(number, source, target, peer):
        return pltpu.make_async_remote_copy(
            src_ref=source, dst_ref=target, send_sem=sum_send.at[number],
            recv_sem=sum_recv.at[number], device_id=peer, device_id_type=MESH,
        )

    base_a = core * half_rows
    base_b = base_a + quad * block_rows
    base_c = base_b + line * chunk
    sb[...] = sums[...].astype(BF16)
    number = 0
    stage = [send(0, sb.at[at((1 - core) * half_rows, half_rows)], in_a, peer_a)]
    stage[0].start()

    top, one, zero = v0, v1, slope

    def project_fine(i, _):
        x = ag[pl.ds(4 * i, 4)].reshape(4 * width, feats)
        wide = (4, width, feats)
        top[pl.ds(4 * i, 4)] = dot_rows(x, w1[2]).astype(BF16).astype(F32).reshape(wide)
        one[pl.ds(4 * i, 4)] = dot_rows(x, w1[1]).reshape(wide)
        zero[pl.ds(4 * i, 4)] = dot_rows(x, w1[0]).reshape(wide)
        return 0

    lax.fori_loop(0, (rows + 4) // 4, project_fine, 0)

    stage[0].wait()
    own = sums[at(base_a, half_rows), :] + in_a[...].astype(F32)
    sums[at(base_a, half_rows), :] = own
    sb[at(base_a, half_rows), :] = own.astype(BF16)
    stage = []
    for j, (q, peer) in enumerate(peers_b):
        number += 1
        stage.append(
            send(number, sb.at[at(base_a + q * block_rows, block_rows)], in_b.at[j], peer)
        )
        stage[-1].start()

    def fine_middle(a, _):
        for half in range(halves):
            lanes = pl.ds(half * LANES, LANES)
            mid[a, :, lanes] = (
                (one[a, :, lanes] + 2.0 * stencil(top, coefs, a, a + 4, half))
                .astype(BF16)
                .astype(F32)
            )
        return 0

    lax.fori_loop(1, rows + 3, fine_middle, 0)

    for copy in stage:
        copy.wait()
    own = sums[at(base_b, block_rows), :]
    for j in range(len(peers_b)):
        own = own + in_b[j].astype(F32)
    sums[at(base_b, block_rows), :] = own
    sb[at(base_b, block_rows), :] = own.astype(BF16)
    stage = []
    for j, (z, peer) in enumerate(peers_c):
        number += 1
        stage.append(send(number, sb.at[at(base_b + z * chunk, chunk)], in_c.at[j], peer))
        stage[-1].start()

    def fine_grad(a, _):
        for half in range(halves):
            lanes = pl.ds(half * LANES, LANES)
            value = (
                zero[a, :, lanes] - top[a, :, lanes] + stencil(mid, coefs, a, a + 4, half)
            )
            gp[a - 2, :, lanes] = value[RIM : RIM + cols].astype(BF16)
        return 0

    lax.fori_loop(2, rows + 2, fine_grad, 0)

    for copy in stage:
        copy.wait()
    own = sums[at(base_c, chunk), :]
    for j in range(len(peers_c)):
        own = own + in_c[j].astype(F32)
    full[at(base_c, chunk), :] = own.astype(BF16)

    stages = (
        (base_c, chunk, [p for _, p in peers_c]),
        (base_b, block_rows, [p for _, p in peers_b]),
        (base_a, half_rows, [peer_a]),
    )
    for start, size, peers in stages:
        stage = []
        for peer in peers:
            number += 1
            region = full.at[at(start, size)]
            stage.append(send(number, region, region, peer))
            stage[-1].start()
        for copy in stage:
            copy.wait()

    squares = jnp.zeros((8, feats), F32)
    for k in range(6):
        x = full[pl.ds(k * feats, feats), :].astype(F32)
        squares = squares + jnp.sum((x * x).reshape(feats // 8, 8, feats), axis=0)
    square_sum = jnp.sum(jnp.sum(squares, axis=0, keepdims=True), axis=1, keepdims=True)
    factor = jnp.minimum(1.0, 2.0 * feats * lax.rsqrt(square_sum + 1e-06))
    for k in range(3):
        rows_k = pl.ds(k * feats, feats)
        gfirst[rows_k, :] = full[rows_k, :].astype(F32) * factor
        gsecond[rows_k, :] = full[pl.ds((3 + k) * feats, feats), :].astype(F32) * factor

    for r in range(prows):
        out = dot(q0[POOL_UP + r], w2[0]) + dot(q1[POOL_UP + r], w2[1])
        out = out + dot(q2[POOL_UP + r], w2[2])
        level[r] = out[RIM : RIM + pcols].astype(BF16)


def shards(groups, members, pixels, offsets, first_weights, second_weights, cotangent):
    rows, cols, feats = pixels.shape
    prows, pcols = cotangent.shape[:2]
    width, pwidth = cols + 2 * RIM, pcols + 2 * RIM
    high, phigh, bhigh = rows + 2 * FINE_UP, prows + 2 * POOL_UP, rows + 4
    count = groups * members
    chunk = -(-6 * feats // (count * 16)) * 16
    total = chunk * count
    half = total // 2
    lines = members // 2
    orders = len(STEPS)

    def blocks(n):
        return -(-orders * n // LANES)

    nf, np_ = blocks(rows + 16), blocks(phigh)
    vm = pltpu.VMEM

    def halo(n, up, c):
        return [
            vm((2, n // 2, 16, feats), BF16),
            vm((2, up, c, feats), BF16),
            vm((2, n // 2, 16, feats), BF16),
            vm((4, up // 2, 16, feats), BF16),
        ]

    scratch = [vm((rows, LANES), F32), vm((orders, rows, LANES), F32)]
    scratch += halo(rows, FINE_UP, cols) + halo(prows, POOL_UP, pcols)
    scratch += [
        vm((rows + 16, LANES), F32),
        vm((nf * LANES, LANES), F32), vm((nf, LANES, LANES), F32),
        vm((np_ * LANES, LANES), F32), vm((np_, LANES, LANES), F32),
        vm((orders, high, width, LANES), F32), vm((orders, phigh, pwidth, LANES), F32),
    ]
    scratch += [vm((high, width, feats), t) for t in (BF16, BF16, BF16, F32, F32)]
    scratch += [vm((rows + 8, width, feats), F32)]
    scratch += [vm((phigh, pwidth, feats), BF16), vm((prows, pwidth, feats), BF16)]
    scratch += [vm((phigh, pwidth, feats), t) for t in (BF16,) * 3 + (F32,) * 7]
    scratch += [vm((bhigh, width, feats), t) for t in (BF16, BF16, F32)]
    scratch += [
        vm((total, feats), F32), vm((total, feats), BF16), vm((total, feats), BF16),
        vm((half, feats), BF16),
        vm((groups - 1, half // groups, feats), BF16),
        vm((lines - 1, chunk, feats), BF16),
    ]
    copies = 2 * (groups + lines - 1)
    scratch += [pltpu.SemaphoreType.DMA((3, orders))] * 2
    scratch += [pltpu.SemaphoreType.DMA((copies,))] * 2
    grad_pixels, first, second, level = pl.pallas_call(
        functools.partial(kernel, groups, members, chunk),
        out_shape=(
            jax.ShapeDtypeStruct(pixels.shape, BF16),
            jax.ShapeDtypeStruct((3 * feats, feats), F32),
            jax.ShapeDtypeStruct((3 * feats, feats), F32),
            jax.ShapeDtypeStruct(cotangent.shape, BF16),
        ),
        in_specs=[pl.BlockSpec(memory_space=pltpu.VMEM)] * 5,
        out_specs=[pl.BlockSpec(memory_space=pltpu.VMEM)] * 4,
        scratch_shapes=scratch,
        compiler_params=pltpu.CompilerParams(
            collective_id=0, has_side_effects=True, vmem_limit_bytes=60 * 1024 * 1024
        ),
    )(pixels, offsets, first_weights, second_weights, cotangent)
    shape = first_weights.shape
    return grad_pixels, first.reshape(shape), second.reshape(shape), level


def solution(mesh):
    groups, members = mesh.shape["grp"], mesh.shape["dev"]
    return jax.shard_map(
        functools.partial(shards, groups, members),
        mesh=mesh,
        in_specs=(P("grp", "dev", None), P("grp", "dev"), P(), P(), P("grp", "dev", None)),
        out_specs=(P("grp", "dev", None), P(), P(), P("grp", "dev", None)),
        check_vma=False,
    )
```

time: 248 us -> 64.8 us (0.26)
  waiting for transfers between devices: 134 us -> 0 us
  Pallas kernels: 0 us -> 58.8 us
  starting transfers between devices: 53.5 us -> 0 us
  between operations: 16.9 us -> 0.65 us
  other arithmetic: 15.3 us -> 0 us
  matrix products: 14.6 us -> 0 us
  local copies, waits for them, and re-layouts: 13.2 us -> 5.05 us
    psum x1 -> x0, waiting for transfers between devices: 125 us -> none  [shards(): lax.psum((first_sum, second_sum), ('grp', 'dev'))]
    pallas_call x0 -> x1, Pallas kernels: none -> 58.8 us  [shards(): pl.pallas_call(functools.partial(kernel, groups, members, chunk), out_sha...]
    ppermute x20 -> x0, starting transfers between devices: 53.4 us -> none  [the longest x10 40.4 us: with_halo(): lax.ppermute(lax.slice_in_dim(block, block.shape[dim] - width, None, axis...]
    dot_general x10 -> x0, matrix products: 14.6 us -> none  [the longest x6 8.25 us: project_back(): jnp.dot(flattened, weights[order_index].T, preferred_element_type=jnp.flo...]
    ppermute x20 -> x0, waiting for transfers between devices: 8.63 us -> none  [the longest x10 8.61 us: with_halo(): lax.ppermute(lax.slice_in_dim(block, 0, width, axis=dim), axis, backward)]
    slice x44 -> x0, local copies, waits for them, and re-layouts: 6.59 us -> none  [the longest x33 2.4 us: trim(): tensor[margin_cut:tensor.shape[0] - margin_cut, margin_cut:tensor.shape[1...]
    mul x8 -> x0, other arithmetic: 6.47 us -> none  [the longest x4 4.34 us: apply_operator(): scaled = root_ext[:, :, None] * extended.astype(jnp.float32)]
    reshape x3 -> x0, local copies, waits for them, and re-layouts: 3.95 us -> none  [the longest x1 2.03 us: shards(): hidden.reshape(shard_rows // 2, 2, shard_cols // 2, 2, channels)]
  transfers between devices with their start and end apart: 21 -> 0, of which waited for: 6 -> 0; matrix products, arithmetic and copies ran while one was open for 11% -> 0% of each run, Pallas kernels for 0% -> 0%
where the time goes in v1:
time: 64.8 us; the launch traced here: 64.5 us
  Pallas kernels  58.8 us (91%)
  local copies, waits for them, and re-layouts  5.05 us (8%)
  between operations  0.65 us (1%)
    pallas_call x1, Pallas kernels, shards(): pl.pallas_call(functools.partial(kernel, groups, members, chunk), out_sha...  58.8 us
    unnamed x10, local copies, waits for them, and re-layouts  5.05 us

profile of v1, /device:TPU:0, one launch (start us, length us, event | category | flops | bytes accessed | tf_op | source)
XLA Modules:
  0.0 64.5 jit_solution(18177572156418816206)
XLA Ops:
  0.6 58.8 %shard_map.84 = (bf16[16,64,256]{2,1,0:T(8,128)(2,1)}, f32[768,256]{1,0:T(8,128)}, f32[768,256]{1,0:T(8,128)}, bf16[8,32,256]{2,1,0:T(8,128)(2,1)}) custom-call(bf16[16,64,256]{2,1,0:T(8,128)(2,1)} %px.1, f32[16,64]{1,0:T(8,128)} %off.1, bf16[3,256,256]{2,1,0:T(8,128)(2,1)} %w1.1, bf16[3,256,256]{2,1,0:T(8,128)(2,1)} %w2.1, bf16[8,32,256]{2,1,0:T(8,128)(2,1)} %cot.1), custom_call_target="tpu_custom_call" | custom-call | tf_op jit(solution)/shard_map/pallas_call | solution.py:614
  59.5 0.0 copy-start.1
  59.5 2.0 %copy.13 = bf16[16,64,256]{2,1,0:T(8,128)(2,1)} copy(bf16[16,64,256]{2,1,0:T(8,128)(2,1)} %get-tuple-element.16) | data formatting | bytes 1048576
  61.4 0.0 copy-done.1
  61.4 0.0 copy-start
  61.4 0.9 %copy.14 = f32[3,256,256]{2,1,0:T(8,128)} copy(f32[3,256,256]{2,1,0:T(8,128)S(1)} %bitcast.3) | data formatting | bytes 1572864
  62.3 0.5 copy-done
  62.9 0.0 copy-start.2
  62.9 0.9 %copy.15 = f32[3,256,256]{2,1,0:T(8,128)} copy(f32[3,256,256]{2,1,0:T(8,128)S(1)} %bitcast.2) | data formatting | bytes 1572864
  63.7 0.1 copy-done.2
  63.9 0.7 %copy.16 = bf16[8,32,256]{2,1,0:T(8,128)(2,1)} copy(bf16[8,32,256]{2,1,0:T(8,128)(2,1)S(1)} %copy-done.2) | data formatting | bytes 262144
Async XLA Ops:
  59.5 2.0 %copy-start.1 = (f32[768,256]{1,0:T(8,128)S(1)}, f32[768,256]{1,0:T(8,128)}, u32[]{:S(2)}) copy-start(f32[768,256]{1,0:T(8,128)} %get-tuple-element.9) | copy-start | bytes 2359300
  61.4 1.4 %copy-start = (f32[768,256]{1,0:T(8,128)S(1)}, f32[768,256]{1,0:T(8,128)}, u32[]{:S(2)}) copy-start(f32[768,256]{1,0:T(8,128)} %get-tuple-element.10) | copy-start | bytes 2359300
  62.9 1.0 %copy-start.2 = (bf16[8,32,256]{2,1,0:T(8,128)(2,1)S(1)}, bf16[8,32,256]{2,1,0:T(8,128)(2,1)}, u32[]{:S(2)}) copy-start(bf16[8,32,256]{2,1,0:T(8,128)(2,1)} %get-tuple-element.19) | copy-start | bytes 393220

commit v2 on v1

--- a/solution.py
+++ b/solution.py
@@ -106,7 +106,7 @@
 def kernel(
     groups, members, chunk,
     px, off, w1, w2, cot,
-    gp, gfirst, gsecond, level,
+    gp, full, level,
     off_own, off_in,
     px_pack, px_v, px_h, px_c,
     ct_pack, ct_v, ct_h, ct_c,
@@ -114,7 +114,7 @@
     t0, t1, t2, v0, v1, slope,
     c0, cm, q0, q1, q2, z0, z1, ptop, pone, pzero, pmid, pgrad,
     ag, agm, mid,
-    sums, sb, full, in_a, in_b, in_c,
+    sums, sb, in_a, in_b, in_c,
     halo_send, halo_recv, sum_send, sum_recv,
 ):
     rows, cols, feats = px.shape
@@ -204,21 +204,25 @@
             )
         return outgoing, incoming
 
+    for a in (2, 1, 0):
+        for dr, dc, exists, peer in around:
+            @pl.when(exists)
+            def _():
+                halo_copies(dr, dc, peer)[0][a]().start()
+
     for dr, dc, exists, peer in around:
-        @pl.when(exists)
-        def _():
-            for copy in reversed(halo_copies(dr, dc, peer)[0]):
-                copy().start()
-
         @pl.when(jnp.logical_not(exists))
         def _():
             for here, _ in halo_copies(dr, dc, peer)[1]:
                 here[...] = jnp.zeros(here.shape, here.dtype)
 
-    for dr, dc, exists, peer in around:
-        @pl.when(exists)
-        def _():
-            halo_copies(dr, dc, peer)[1][2][1]().wait_recv()
+    def receive(a):
+        for dr, dc, exists, peer in around:
+            @pl.when(exists)
+            def _():
+                halo_copies(dr, dc, peer)[1][a][1]().wait_recv()
+
+    receive(2)
 
     def lay(left, own, right):
         lane = lax.broadcasted_iota(jnp.int32, own.shape, 1)
@@ -246,9 +250,6 @@
     offsets = off_ext[...]
     inside = within(
         offsets.shape, g * rows - 8, d * cols - RIM, groups * rows, members * cols, width
-    )
-    spread_coefficients(
-        edge_coefficients(offsets, inside), stack, turned, coefs, 2, 1, rows + 2 * FINE_UP - 1
     )
     pshape = (prows + 2 * POOL_UP, LANES)
     a_r = lax.broadcasted_iota(jnp.int32, (pshape[0], rows + 16), 0)
@@ -269,15 +270,6 @@
         prows + 2 * POOL_UP - 1,
     )
 
-    for dr, dc, exists, peer in around:
-        @pl.when(exists)
-        def _():
-            outgoing, incoming = halo_copies(dr, dc, peer)
-            for _, copy in incoming[:2]:
-                copy().wait_recv()
-            for copy in outgoing:
-                copy().wait_send()
-
     def assemble(store, start, pairs, middle, left, right):
         def pair(i, _):
             lt, rt = left(i).astype(F32), right(i).astype(F32)
@@ -302,14 +294,51 @@
     def store_cot(e, row):
         c0[e] = row.astype(BF16)
 
-    for store, src, up, v, h, c in (
-        (store_px, px, FINE_UP, px_v, px_h, px_c),
-        (store_cot, cot, POOL_UP, ct_v, ct_h, ct_c),
-    ):
+    def assemble_all(store, src, up, v, h, c):
         n = src.shape[0]
         assemble(store, 0, up // 2, lambda r: v[0, r], lambda i: c[0, i], lambda i: c[1, i])
         assemble(store, up, n // 2, lambda r: src[r], lambda i: h[0, i], lambda i: h[1, i])
         assemble(store, up + n, up // 2, lambda r: v[1, r], lambda i: c[2, i], lambda i: c[3, i])
+
+    receive(1)
+    assemble_all(store_cot, cot, POOL_UP, ct_v, ct_h, ct_c)
+
+    def project_pool(i, _):
+        x = c0[pl.ds(4 * i, 4)].reshape(4 * pwidth, feats)
+        wide = (4, pwidth, feats)
+        ptop[pl.ds(4 * i, 4)] = dot_rows(x, w2[2]).astype(BF16).astype(F32).reshape(wide)
+        pone[pl.ds(4 * i, 4)] = dot_rows(x, w2[1]).reshape(wide)
+        pzero[pl.ds(4 * i, 4)] = dot_rows(x, w2[0]).reshape(wide)
+        return 0
+
+    lax.fori_loop(0, (prows + 2 * POOL_UP) // 4, project_pool, 0)
+
+    def pool_middle(e, _):
+        for half in range(halves):
+            lanes = pl.ds(half * LANES, LANES)
+            pmid[e, :, lanes] = (
+                (pone[e, :, lanes] + 2.0 * stencil(ptop, pcoefs, e, e, half))
+                .astype(BF16)
+                .astype(F32)
+            )
+        return 0
+
+    def pool_grad(e, _):
+        for half in range(halves):
+            lanes = pl.ds(half * LANES, LANES)
+            pgrad[e, :, lanes] = (
+                pzero[e, :, lanes] - ptop[e, :, lanes] + stencil(pmid, pcoefs, e, e, half)
+            )
+        return 0
+
+    lax.fori_loop(2, prows + 2 * POOL_UP - 2, pool_middle, 0)
+    lax.fori_loop(3, prows + 2 * POOL_UP - 3, pool_grad, 0)
+
+    spread_coefficients(
+        edge_coefficients(offsets, inside), stack, turned, coefs, 2, 1, rows + 2 * FINE_UP - 1
+    )
+    receive(0)
+    assemble_all(store_px, px, FINE_UP, px_v, px_h, px_c)
 
     def fine_one(e, _):
         for half in range(halves):
@@ -358,37 +387,6 @@
 
     lax.fori_loop(0, (prows + 4) // 2, activate, 0)
 
-    def project_pool(i, _):
-        x = c0[pl.ds(4 * i, 4)].reshape(4 * pwidth, feats)
-        wide = (4, pwidth, feats)
-        ptop[pl.ds(4 * i, 4)] = dot_rows(x, w2[2]).astype(BF16).astype(F32).reshape(wide)
-        pone[pl.ds(4 * i, 4)] = dot_rows(x, w2[1]).reshape(wide)
-        pzero[pl.ds(4 * i, 4)] = dot_rows(x, w2[0]).reshape(wide)
-        return 0
-
-    lax.fori_loop(0, (prows + 2 * POOL_UP) // 4, project_pool, 0)
-
-    def pool_middle(e, _):
-        for half in range(halves):
-            lanes = pl.ds(half * LANES, LANES)
-            pmid[e, :, lanes] = (
-                (pone[e, :, lanes] + 2.0 * stencil(ptop, pcoefs, e, e, half))
-                .astype(BF16)
-                .astype(F32)
-            )
-        return 0
-
-    def pool_grad(e, _):
-        for half in range(halves):
-            lanes = pl.ds(half * LANES, LANES)
-            pgrad[e, :, lanes] = (
-                pzero[e, :, lanes] - ptop[e, :, lanes] + stencil(pmid, pcoefs, e, e, half)
-            )
-        return 0
-
-    lax.fori_loop(2, prows + 2 * POOL_UP - 2, pool_middle, 0)
-    lax.fori_loop(3, prows + 2 * POOL_UP - 3, pool_grad, 0)
-
     col = lax.broadcasted_iota(jnp.int32, (width, feats), 0)
     own_cols = (col >= RIM) & (col < cols + RIM)
 
@@ -418,51 +416,118 @@
             ).astype(BF16)
         return 0
 
-    lax.fori_loop(POOL_UP - 1, prows + POOL_UP + 1, pool_one, 0)
-    lax.fori_loop(POOL_UP, prows + POOL_UP, pool_two, 0)
-
-    pcol = lax.broadcasted_iota(jnp.int32, (pwidth, feats), 0)
-    own_pcols = (pcol >= RIM) & (pcol < pcols + RIM)
-
-    def mask_cot(r, _):
-        cm[r] = jnp.where(own_pcols, c0[POOL_UP + r].astype(F32), 0.0).astype(BF16)
-        return 0
-
-    lax.fori_loop(0, prows, mask_cot, 0)
-
-    if sums.shape[0] > 6 * feats:
-        sums[pl.ds(6 * feats, sums.shape[0] - 6 * feats), :] = jnp.zeros(
-            (sums.shape[0] - 6 * feats, feats), F32
-        )
-    back = agm[pl.ds(2, rows)].reshape(rows * width, feats)
-    for k, term in enumerate((t0, t1, t2)):
-        x = term[pl.ds(FINE_UP, rows)].reshape(rows * width, feats)
-        sums[pl.ds(k * feats, feats), :] = dot_sum(x, back)
-    pback = cm[...].reshape(prows * pwidth, feats)
-    for k, term in enumerate((q0, q1, q2)):
-        x = term[pl.ds(POOL_UP, prows)].reshape(prows * pwidth, feats)
-        sums[pl.ds((3 + k) * feats, feats), :] = dot_sum(x, pback)
-
-    total = sums.shape[0]
-    half_rows = total // 2
+    batch = sums.shape[0] // 2
+    half_rows = batch // 2
     block_rows = half_rows // groups
+    parts = 3 * feats * halves
 
     def at(start, size):
         return pl.ds(pl.multiple_of(start, 16), size)
 
-    def send(number, source, target, peer):
-        return pltpu.make_async_remote_copy(
+    numbers = iter(range(sum_send.shape[0]))
+
+    def send(source, target, peer):
+        number = next(numbers)
+        copy = pltpu.make_async_remote_copy(
             src_ref=source, dst_ref=target, send_sem=sum_send.at[number],
             recv_sem=sum_recv.at[number], device_id=peer, device_id_type=MESH,
         )
-
-    base_a = core * half_rows
-    base_b = base_a + quad * block_rows
-    base_c = base_b + line * chunk
-    sb[...] = sums[...].astype(BF16)
-    number = 0
-    stage = [send(0, sb.at[at((1 - core) * half_rows, half_rows)], in_a, peer_a)]
-    stage[0].start()
+        copy.start()
+        return copy
+
+    def starts(t):
+        base_a = t * batch + core * half_rows
+        base_b = base_a + quad * block_rows
+        return base_a, base_b, base_b + line * chunk
+
+    def patch_sums(t, terms, first, count, back):
+        if batch > parts:
+            rest = batch - parts
+            sb[pl.ds(t * batch + parts, rest), :] = jnp.zeros((rest, LANES), BF16)
+            sums[pl.ds(t * batch + parts, rest), :] = jnp.zeros((rest, LANES), F32)
+        for k, term in enumerate(terms):
+            x = term[pl.ds(first, count)].reshape(back.shape[0], feats)
+            value = dot_sum(x, back)
+            for half in range(halves):
+                place = pl.ds(t * batch + (half * 3 + k) * feats, feats)
+                part = value[:, half * LANES : (half + 1) * LANES]
+                sums[place, :] = part
+                sb[place, :] = part.astype(BF16)
+
+    def start_a(t):
+        other = at(t * batch + (1 - core) * half_rows, half_rows)
+        return [send(sb.at[other], in_a.at[t], peer_a)]
+
+    def add(copies, start, size, landed):
+        for copy in copies:
+            copy.wait()
+        own = sums[at(start, size), :]
+        for j in range(len(copies)):
+            own = own + landed(j).astype(F32)
+        return own
+
+    def a_to_b(t, copies):
+        base_a, base_b, _ = starts(t)
+        own = add(copies, base_a, half_rows, lambda j: in_a[t])
+        sums[at(base_a, half_rows), :] = own
+        sb[at(base_a, half_rows), :] = own.astype(BF16)
+        return [
+            send(sb.at[at(base_a + q * block_rows, block_rows)], in_b.at[t, j], peer)
+            for j, (q, peer) in enumerate(peers_b)
+        ]
+
+    def b_to_c(t, copies):
+        _, base_b, _ = starts(t)
+        own = add(copies, base_b, block_rows, lambda j: in_b[t, j])
+        sums[at(base_b, block_rows), :] = own
+        sb[at(base_b, block_rows), :] = own.astype(BF16)
+        return [
+            send(sb.at[at(base_b + z * chunk, chunk)], in_c.at[t, j], peer)
+            for j, (z, peer) in enumerate(peers_c)
+        ]
+
+    def c_to_c(t, copies):
+        base_c = starts(t)[2]
+        full[at(base_c, chunk), :] = add(
+            copies, base_c, chunk, lambda j: in_c[t, j]
+        ).astype(BF16)
+        region = full.at[at(base_c, chunk)]
+        return [send(region, region, peer) for _, peer in peers_c]
+
+    def c_to_b(t, copies):
+        for copy in copies:
+            copy.wait()
+        region = full.at[at(starts(t)[1], block_rows)]
+        return [send(region, region, peer) for _, peer in peers_b], send(region, region, peer_a)
+
+    def b_to_a(t, copies):
+        copies, first = copies
+        onward = [first]
+        for j, copy in enumerate(copies):
+            copy.wait()
+            came = lax.rem(quad + groups - 1 - j, groups)
+            region = full.at[at(starts(t)[0] + came * block_rows, block_rows)]
+            onward.append(send(region, region, peer_a))
+        return onward
+
+    back = agm[pl.ds(2, rows)].reshape(rows * width, feats)
+    patch_sums(0, (t0, t1, t2), FINE_UP, rows, back)
+    fine = start_a(0)
+
+    lax.fori_loop(POOL_UP - 1, prows + POOL_UP + 1, pool_one, 0)
+    fine = a_to_b(0, fine)
+    lax.fori_loop(POOL_UP, prows + POOL_UP, pool_two, 0)
+    pcol = lax.broadcasted_iota(jnp.int32, (pwidth, feats), 0)
+    own_pcols = (pcol >= RIM) & (pcol < pcols + RIM)
+
+    def mask_cot(r, _):
+        cm[r] = jnp.where(own_pcols, c0[POOL_UP + r].astype(F32), 0.0).astype(BF16)
+        return 0
+
+    lax.fori_loop(0, prows, mask_cot, 0)
+
+    patch_sums(1, (q0, q1, q2), POOL_UP, prows, cm[...].reshape(prows * pwidth, feats))
+    pool = start_a(1)
 
     top, one, zero = v0, v1, slope
 
@@ -474,20 +539,6 @@
         zero[pl.ds(4 * i, 4)] = dot_rows(x, w1[0]).reshape(wide)
         return 0
 
-    lax.fori_loop(0, (rows + 4) // 4, project_fine, 0)
-
-    stage[0].wait()
-    own = sums[at(base_a, half_rows), :] + in_a[...].astype(F32)
-    sums[at(base_a, half_rows), :] = own
-    sb[at(base_a, half_rows), :] = own.astype(BF16)
-    stage = []
-    for j, (q, peer) in enumerate(peers_b):
-        number += 1
-        stage.append(
-            send(number, sb.at[at(base_a + q * block_rows, block_rows)], in_b.at[j], peer)
-        )
-        stage[-1].start()
-
     def fine_middle(a, _):
         for half in range(halves):
             lanes = pl.ds(half * LANES, LANES)
@@ -498,21 +549,6 @@
             )
         return 0
 
-    lax.fori_loop(1, rows + 3, fine_middle, 0)
-
-    for copy in stage:
-        copy.wait()
-    own = sums[at(base_b, block_rows), :]
-    for j in range(len(peers_b)):
-        own = own + in_b[j].astype(F32)
-    sums[at(base_b, block_rows), :] = own
-    sb[at(base_b, block_rows), :] = own.astype(BF16)
-    stage = []
-    for j, (z, peer) in enumerate(peers_c):
-        number += 1
-        stage.append(send(number, sb.at[at(base_b + z * chunk, chunk)], in_c.at[j], peer))
-        stage[-1].start()
-
     def fine_grad(a, _):
         for half in range(halves):
             lanes = pl.ds(half * LANES, LANES)
@@ -522,45 +558,54 @@
             gp[a - 2, :, lanes] = value[RIM : RIM + cols].astype(BF16)
         return 0
 
-    lax.fori_loop(2, rows + 2, fine_grad, 0)
-
-    for copy in stage:
+    lax.fori_loop(0, (rows + 4) // 4, project_fine, 0)
+    pool = a_to_b(1, pool)
+    fine = b_to_c(0, fine)
+    lax.fori_loop(1, rows + 3, fine_middle, 0)
+    fine = c_to_c(0, fine)
+    pool = b_to_c(1, pool)
+    lax.fori_loop(2, rows // 2 + 2, fine_grad, 0)
+    fine = c_to_b(0, fine)
+    pool = c_to_c(1, pool)
+    lax.fori_loop(rows // 2 + 2, rows + 2, fine_grad, 0)
+    pool = c_to_b(1, pool)
+
+    flat = (prows * pwidth, feats)
+    out = dot(q0[pl.ds(POOL_UP, prows)].reshape(flat), w2[0])
+    out = out + dot(q1[pl.ds(POOL_UP, prows)].reshape(flat), w2[1])
+    out = out + dot(q2[pl.ds(POOL_UP, prows)].reshape(flat), w2[2])
+    for r in range(prows):
+        start = r * pwidth + RIM
+        level[r] = out[start : start + pcols].astype(BF16)
+
+    fine = b_to_a(0, fine)
+    pool = b_to_a(1, pool)
+    for copy in fine + pool:
         copy.wait()
-    own = sums[at(base_c, chunk), :]
-    for j in range(len(peers_c)):
-        own = own + in_c[j].astype(F32)
-    full[at(base_c, chunk), :] = own.astype(BF16)
-
-    stages = (
-        (base_c, chunk, [p for _, p in peers_c]),
-        (base_b, block_rows, [p for _, p in peers_b]),
-        (base_a, half_rows, [peer_a]),
-    )
-    for start, size, peers in stages:
-        stage = []
-        for peer in peers:
-            number += 1
-            region = full.at[at(start, size)]
-            stage.append(send(number, region, region, peer))
-            stage[-1].start()
-        for copy in stage:
-            copy.wait()
-
-    squares = jnp.zeros((8, feats), F32)
-    for k in range(6):
-        x = full[pl.ds(k * feats, feats), :].astype(F32)
-        squares = squares + jnp.sum((x * x).reshape(feats // 8, 8, feats), axis=0)
+    for dr, dc, exists, peer in around:
+        @pl.when(exists)
+        def _():
+            for copy in halo_copies(dr, dc, peer)[0]:
+                copy().wait_send()
+
+
+def finish(full, gp, level, gp_out, gfirst, gsecond, level_out):
+    feats = gfirst.shape[1]
+    halves = feats // LANES
+    batch = full.shape[0] // 2
+    count = gfirst.shape[0]
+    gp_out[...] = gp[...]
+    level_out[...] = level[...]
+    squares = jnp.zeros((8, LANES), F32)
+    for t in range(2):
+        x = full[pl.ds(t * batch, count * halves), :].astype(F32)
+        squares = squares + jnp.sum((x * x).reshape(count * halves // 8, 8, LANES), axis=0)
     square_sum = jnp.sum(jnp.sum(squares, axis=0, keepdims=True), axis=1, keepdims=True)
     factor = jnp.minimum(1.0, 2.0 * feats * lax.rsqrt(square_sum + 1e-06))
-    for k in range(3):
-        rows_k = pl.ds(k * feats, feats)
-        gfirst[rows_k, :] = full[rows_k, :].astype(F32) * factor
-        gsecond[rows_k, :] = full[pl.ds((3 + k) * feats, feats), :].astype(F32) * factor
-
-    for r in range(prows):
-        out = dot(q0[POOL_UP + r], w2[0]) + dot(q1[POOL_UP + r], w2[1])
-        out = out + dot(q2[POOL_UP + r], w2[2])
-        level[r] = out[RIM : RIM + pcols].astype(BF16)
+    for t, out in enumerate((gfirst, gsecond)):
+        for half in range(halves):
+            x = full[pl.ds(t * batch + half * count, count), :].astype(F32)
+            out[:, pl.ds(half * LANES, LANES)] = x * factor
 
 
 def shards(groups, members, pixels, offsets, first_weights, second_weights, cotangent):
@@ -569,7 +614,7 @@
     width, pwidth = cols + 2 * RIM, pcols + 2 * RIM
     high, phigh, bhigh = rows + 2 * FINE_UP, prows + 2 * POOL_UP, rows + 4
     count = groups * members
-    chunk = -(-6 * feats // (count * 16)) * 16
+    chunk = -(-3 * feats * (feats // LANES) // (count * 16)) * 16
     total = chunk * count
     half = total // 2
     lines = members // 2
@@ -603,29 +648,40 @@
     scratch += [vm((phigh, pwidth, feats), t) for t in (BF16,) * 3 + (F32,) * 7]
     scratch += [vm((bhigh, width, feats), t) for t in (BF16, BF16, F32)]
     scratch += [
-        vm((total, feats), F32), vm((total, feats), BF16), vm((total, feats), BF16),
-        vm((half, feats), BF16),
-        vm((groups - 1, half // groups, feats), BF16),
-        vm((lines - 1, chunk, feats), BF16),
+        vm((2 * total, LANES), F32), vm((2 * total, LANES), BF16),
+        vm((2, half, LANES), BF16),
+        vm((2, groups - 1, half // groups, LANES), BF16),
+        vm((2, lines - 1, chunk, LANES), BF16),
     ]
-    copies = 2 * (groups + lines - 1)
     scratch += [pltpu.SemaphoreType.DMA((3, orders))] * 2
+    copies = 2 * (3 * groups + 2 * lines - 3)
     scratch += [pltpu.SemaphoreType.DMA((copies,))] * 2
+    inner_pixels, full, inner_level = pl.pallas_call(
+        functools.partial(kernel, groups, members, chunk),
+        out_shape=(
+            jax.ShapeDtypeStruct(pixels.shape, BF16),
+            jax.ShapeDtypeStruct((2 * total, LANES), BF16),
+            jax.ShapeDtypeStruct(cotangent.shape, BF16),
+        ),
+        in_specs=[pl.BlockSpec(memory_space=pltpu.VMEM)] * 5,
+        out_specs=[pl.BlockSpec(memory_space=pltpu.VMEM)] * 3,
+        scratch_shapes=scratch,
+        compiler_params=pltpu.CompilerParams(
+            collective_id=0, has_side_effects=True, vmem_limit_bytes=60 * 1024 * 1024
+        ),
+    )(pixels, offsets, first_weights, second_weights, cotangent)
     grad_pixels, first, second, level = pl.pallas_call(
-        functools.partial(kernel, groups, members, chunk),
+        finish,
         out_shape=(
             jax.ShapeDtypeStruct(pixels.shape, BF16),
             jax.ShapeDtypeStruct((3 * feats, feats), F32),
             jax.ShapeDtypeStruct((3 * feats, feats), F32),
             jax.ShapeDtypeStruct(cotangent.shape, BF16),
         ),
-        in_specs=[pl.BlockSpec(memory_space=pltpu.VMEM)] * 5,
+        in_specs=[pl.BlockSpec(memory_space=pltpu.VMEM)] * 3,
         out_specs=[pl.BlockSpec(memory_space=pltpu.VMEM)] * 4,
-        scratch_shapes=scratch,
-        compiler_params=pltpu.CompilerParams(
-            collective_id=0, has_side_effects=True, vmem_limit_bytes=60 * 1024 * 1024
-        ),
-    )(pixels, offsets, first_weights, second_weights, cotangent)
+        compiler_params=pltpu.CompilerParams(vmem_limit_bytes=40 * 1024 * 1024),
+    )(full, inner_pixels, inner_level)
     shape = first_weights.shape
     return grad_pixels, first.reshape(shape), second.reshape(shape), level
 

time: 64.8 us -> 59.2 us (0.914)
  Pallas kernels: 58.8 us -> 55.2 us
  local copies, waits for them, and re-layouts: 5.05 us -> 3.07 us
    pallas_call x1, Pallas kernels: 58.8 us -> 53.7 us  [shards(): pl.pallas_call(functools.partial(kernel, groups, members, chunk), out_sha...]
    unnamed x10 -> x6, local copies, waits for them, and re-layouts: 5.05 us -> 3.07 us
    pallas_call x0 -> x1, Pallas kernels: none -> 1.56 us  [shards(): pl.pallas_call(finish, out_shape=(jax.ShapeDtypeStruct(pixels.shape, BF16...]
where the time goes in v2:
time: 59.2 us; the launch traced here: 59 us
  Pallas kernels  55.2 us (93%)
  local copies, waits for them, and re-layouts  3.07 us (5%)
  between operations  0.65 us (1%)
    pallas_call x1, Pallas kernels, shards(): pl.pallas_call(functools.partial(kernel, groups, members, chunk), out_sha...  53.7 us
    unnamed x6, local copies, waits for them, and re-layouts  3.07 us
    pallas_call x1, Pallas kernels, shards(): pl.pallas_call(finish, out_shape=(jax.ShapeDtypeStruct(pixels.shape, BF16...  1.56 us

profile of v2, /device:TPU:0, one launch (start us, length us, event | category | flops | bytes accessed | tf_op | source)
XLA Modules:
  0.0 59.0 jit_solution(16767688180486079405)
XLA Ops:
  0.6 53.7 %shard_map.84 = (bf16[16,64,256]{2,1,0:T(8,128)(2,1)}, bf16[3072,128]{1,0:T(8,128)(2,1)}, bf16[8,32,256]{2,1,0:T(8,128)(2,1)}) custom-call(bf16[16,64,256]{2,1,0:T(8,128)(2,1)} %px.1, f32[16,64]{1,0:T(8,128)} %off.1, bf16[3,256,256]{2,1,0:T(8,128)(2,1)} %w1.1, bf16[3,256,256]{2,1,0:T(8,128)(2,1)} %w2.1, bf16[8,32,256]{2,1,0:T(8,128)(2,1)} %cot.1), custom_call_target="tpu_custom_call" | custom-call | tf_op jit(solution)/shard_map/pallas_call | solution.py:659
  54.3 0.0 copy-start
  54.3 1.1 %copy-done = bf16[3072,128]{1,0:T(8,128)(2,1)S(1)} copy-done((bf16[3072,128]{1,0:T(8,128)(2,1)S(1)}, bf16[3072,128]{1,0:T(8,128)(2,1)}, u32[]{:S(2)}) %copy-start) | copy-done | bytes 786456
  55.5 0.0 copy-start.1
  55.5 1.0 %copy-done.1 = bf16[16,64,256]{2,1,0:T(8,128)(2,1)S(1)} copy-done((bf16[16,64,256]{2,1,0:T(8,128)(2,1)S(1)}, bf16[16,64,256]{2,1,0:T(8,128)(2,1)}, u32[]{:S(2)}) %copy-start.1) | copy-done | bytes 524312
  56.5 0.0 copy-start.2
  56.5 0.9 %copy-done.2 = bf16[8,32,256]{2,1,0:T(8,128)(2,1)S(1)} copy-done((bf16[8,32,256]{2,1,0:T(8,128)(2,1)S(1)}, bf16[8,32,256]{2,1,0:T(8,128)(2,1)}, u32[]{:S(2)}) %copy-start.2) | copy-done | bytes 131096
  57.4 1.6 %shard_map.85 = (bf16[16,64,256]{2,1,0:T(8,128)(2,1)}, f32[768,256]{1,0:T(8,128)}, f32[768,256]{1,0:T(8,128)}, bf16[8,32,256]{2,1,0:T(8,128)(2,1)}) custom-call(bf16[3072,128]{1,0:T(8,128)(2,1)S(1)} %copy-done, bf16[16,64,256]{2,1,0:T(8,128)(2,1)S(1)} %copy-done.1, bf16[8,32,256]{2,1,0:T(8,128)(2,1)S(1)} %copy-done.2), custom_call_target="tpu_custom_call" | custom-call | tf_op jit(solution)/shard_map/pallas_call | solution.py:673
Async XLA Ops:
  54.3 1.1 %copy-start = (bf16[3072,128]{1,0:T(8,128)(2,1)S(1)}, bf16[3072,128]{1,0:T(8,128)(2,1)}, u32[]{:S(2)}) copy-start(bf16[3072,128]{1,0:T(8,128)(2,1)} %get-tuple-element.11.full) | copy-start | bytes 2359300
  55.5 1.0 %copy-start.1 = (bf16[16,64,256]{2,1,0:T(8,128)(2,1)S(1)}, bf16[16,64,256]{2,1,0:T(8,128)(2,1)}, u32[]{:S(2)}) copy-start(bf16[16,64,256]{2,1,0:T(8,128)(2,1)} %get-tuple-element.12.gp) | copy-start | bytes 1572868
  56.5 0.9 %copy-start.2 = (bf16[8,32,256]{2,1,0:T(8,128)(2,1)S(1)}, bf16[8,32,256]{2,1,0:T(8,128)(2,1)}, u32[]{:S(2)}) copy-start(bf16[8,32,256]{2,1,0:T(8,128)(2,1)} %get-tuple-element.13.level) | copy-start | bytes 393220

commit v3 on v2

--- a/solution.py
+++ b/solution.py
@@ -85,22 +85,35 @@
     return pltpu.roll(column(-1), 1, 0) + column(0) + pltpu.roll(column(1), width - 1, 0)
 
 
+def by_rows(first, last, work):
+    def two(i, _):
+        e = first + 2 * i
+        for store in work(e) + work(e + 1):
+            store()
+        return 0
+
+    lax.fori_loop(0, (last - first) // 2, two, 0)
+    if (last - first) % 2:
+        for store in work(last - 1):
+            store()
+
+
+def storing(ref, index, value):
+    def store():
+        ref[index] = value.astype(ref.dtype)
+
+    return store
+
+
 def dot(a, b):
     return lax.dot_general(a, b, (((1,), (0,)), ((), ())), preferred_element_type=F32)
 
 
-def dot_rows(a, b):
-    return lax.dot_general(a, b, (((1,), (1,)), ((), ())), preferred_element_type=F32)
-
-
-def dot_sum(a, b):
-    return lax.dot_general(a, b, (((0,), (0,)), ((), ())), preferred_element_type=F32)
-
-
-def split_dot(matrix, value):
+def split_dot(matrix, values):
+    value = jnp.concatenate(values, axis=1)
     high = value.astype(BF16)
     low = (value - high.astype(F32)).astype(BF16)
-    return dot(matrix, high) + dot(matrix, low)
+    return dot(matrix, jnp.concatenate([high, low], axis=0))
 
 
 def kernel(
@@ -113,7 +126,7 @@
     off_ext, stack, turned, pstack, pturned, coefs, pcoefs,
     t0, t1, t2, v0, v1, slope,
     c0, cm, q0, q1, q2, z0, z1, ptop, pone, pzero, pmid, pgrad,
-    ag, agm, mid,
+    ag, agm, mid, w1t, w2t, turned_back,
     sums, sb, in_a, in_b, in_c,
     halo_send, halo_recv, sum_send, sum_recv,
 ):
@@ -222,6 +235,9 @@
             def _():
                 halo_copies(dr, dc, peer)[1][a][1]().wait_recv()
 
+    for source, target in ((w2, w2t), (w1, w1t)):
+        for k in range(source.shape[0]):
+            target[:, pl.ds(k * feats, feats)] = source[k].T
     receive(2)
 
     def lay(left, own, right):
@@ -304,35 +320,33 @@
     assemble_all(store_cot, cot, POOL_UP, ct_v, ct_h, ct_c)
 
     def project_pool(i, _):
-        x = c0[pl.ds(4 * i, 4)].reshape(4 * pwidth, feats)
+        y = dot(c0[pl.ds(4 * i, 4)].reshape(4 * pwidth, feats), w2t[...])
         wide = (4, pwidth, feats)
-        ptop[pl.ds(4 * i, 4)] = dot_rows(x, w2[2]).astype(BF16).astype(F32).reshape(wide)
-        pone[pl.ds(4 * i, 4)] = dot_rows(x, w2[1]).reshape(wide)
-        pzero[pl.ds(4 * i, 4)] = dot_rows(x, w2[0]).reshape(wide)
+        ptop[pl.ds(4 * i, 4)] = y[:, 2 * feats :].astype(BF16).astype(F32).reshape(wide)
+        pone[pl.ds(4 * i, 4)] = y[:, feats : 2 * feats].reshape(wide)
+        pzero[pl.ds(4 * i, 4)] = y[:, :feats].reshape(wide)
         return 0
 
     lax.fori_loop(0, (prows + 2 * POOL_UP) // 4, project_pool, 0)
 
-    def pool_middle(e, _):
-        for half in range(halves):
-            lanes = pl.ds(half * LANES, LANES)
-            pmid[e, :, lanes] = (
-                (pone[e, :, lanes] + 2.0 * stencil(ptop, pcoefs, e, e, half))
-                .astype(BF16)
-                .astype(F32)
-            )
-        return 0
-
-    def pool_grad(e, _):
-        for half in range(halves):
-            lanes = pl.ds(half * LANES, LANES)
-            pgrad[e, :, lanes] = (
-                pzero[e, :, lanes] - ptop[e, :, lanes] + stencil(pmid, pcoefs, e, e, half)
-            )
-        return 0
-
-    lax.fori_loop(2, prows + 2 * POOL_UP - 2, pool_middle, 0)
-    lax.fori_loop(3, prows + 2 * POOL_UP - 3, pool_grad, 0)
+    def pool_middle(e):
+        stores = []
+        for half in range(halves):
+            at_half = (e, slice(None), pl.ds(half * LANES, LANES))
+            value = (pone[at_half] + 2.0 * stencil(ptop, pcoefs, e, e, half)).astype(BF16)
+            stores += [storing(pmid, at_half, value)]
+        return stores
+
+    def pool_grad(e):
+        stores = []
+        for half in range(halves):
+            at_half = (e, slice(None), pl.ds(half * LANES, LANES))
+            value = pzero[at_half] - ptop[at_half] + stencil(pmid, pcoefs, e, e, half)
+            stores += [storing(pgrad, at_half, value)]
+        return stores
+
+    by_rows(2, prows + 2 * POOL_UP - 2, pool_middle)
+    by_rows(3, prows + 2 * POOL_UP - 3, pool_grad)
 
     spread_coefficients(
         edge_coefficients(offsets, inside), stack, turned, coefs, 2, 1, rows + 2 * FINE_UP - 1
@@ -340,31 +354,33 @@
     receive(0)
     assemble_all(store_px, px, FINE_UP, px_v, px_h, px_c)
 
-    def fine_one(e, _):
-        for half in range(halves):
+    def fine_one(e):
+        stores = []
+        for half in range(halves):
+            at_half = (e, slice(None), pl.ds(half * LANES, LANES))
             value = stencil(v0, coefs, e, e, half).astype(BF16)
-            t1[e, :, pl.ds(half * LANES, LANES)] = value
-            v1[e, :, pl.ds(half * LANES, LANES)] = value.astype(F32)
-        return 0
-
-    def fine_two(e, _):
-        for half in range(halves):
-            lanes = pl.ds(half * LANES, LANES)
-            t2[e, :, lanes] = (
-                2.0 * stencil(v1, coefs, e, e, half) - v0[e, :, lanes]
-            ).astype(BF16)
-        return 0
-
-    lax.fori_loop(1, rows + 2 * FINE_UP - 1, fine_one, 0)
-    lax.fori_loop(2, rows + 2 * FINE_UP - 2, fine_two, 0)
-
-    def pool_matrix(shape, fine_dim):
+            stores += [storing(t1, at_half, value), storing(v1, at_half, value)]
+        return stores
+
+    def fine_two(e):
+        stores = []
+        for half in range(halves):
+            at_half = (e, slice(None), pl.ds(half * LANES, LANES))
+            value = 2.0 * stencil(v1, coefs, e, e, half) - v0[at_half]
+            stores += [storing(t2, at_half, value)]
+        return stores
+
+    by_rows(1, rows + 2 * FINE_UP - 1, fine_one)
+    by_rows(2, rows + 2 * FINE_UP - 2, fine_two)
+
+    def pool_matrix(shape, fine_dim, repeat):
         f = lax.broadcasted_iota(jnp.int32, shape, fine_dim)
         p = lax.broadcasted_iota(jnp.int32, shape, 1 - fine_dim)
+        f, p = (lax.rem(f, repeat), p) if fine_dim else (f, lax.rem(p, repeat))
         return jnp.where((f == 2 * p - 8) | (f == 2 * p - 7), 0.25, 0.0).astype(BF16)
 
-    gather_pool = pool_matrix((pwidth, width), 1)
-    spread_pool = pool_matrix((width, pwidth), 0)
+    gather_pool = pool_matrix((pwidth, 2 * width), 1, width)
+    spread_pool = pool_matrix((width, 2 * pwidth), 0, pwidth)
 
     def activate(i, _):
         e = 2 + 4 * i
@@ -375,14 +391,16 @@
         s = jax.nn.sigmoid(a)
         slope[pl.ds(4 * i, 4)] = (s * (1.0 + a * (1.0 - s))).reshape(4, width, feats)
         hidden = a * s
+        both = [
+            hidden[2 * p * width : (2 * p + 1) * width]
+            + hidden[(2 * p + 1) * width : (2 * p + 2) * width]
+            for p in (0, 1)
+        ]
+        value = split_dot(gather_pool, both).astype(BF16)
         for p in (0, 1):
-            both = (
-                hidden[2 * p * width : (2 * p + 1) * width]
-                + hidden[(2 * p + 1) * width : (2 * p + 2) * width]
-            )
-            value = split_dot(gather_pool, both).astype(BF16)
-            q0[2 + 2 * i + p] = value
-            z0[2 + 2 * i + p] = value.astype(F32)
+            part = value[:, p * feats : (p + 1) * feats]
+            q0[2 + 2 * i + p] = part
+            z0[2 + 2 * i + p] = part.astype(F32)
         return 0
 
     lax.fori_loop(0, (prows + 4) // 2, activate, 0)
@@ -391,30 +409,30 @@
     own_cols = (col >= RIM) & (col < cols + RIM)
 
     def act_grad(i, _):
-        wide = split_dot(spread_pool, pgrad[i + 3])
-        for s in (0, 1):
-            value = wide * slope[2 * i + 2 + s]
-            ag[2 * i + s] = value.astype(BF16)
-            agm[2 * i + s] = jnp.where(own_cols, value, 0.0).astype(BF16)
+        wide = split_dot(spread_pool, [pgrad[3 + 2 * i], pgrad[4 + 2 * i]])
+        for r in range(4):
+            value = wide[:, (r // 2) * feats : (r // 2 + 1) * feats] * slope[4 * i + 2 + r]
+            ag[4 * i + r] = value.astype(BF16)
+            agm[4 * i + r] = jnp.where(own_cols, value, 0.0).astype(BF16)
         return 0
 
-    lax.fori_loop(0, prows + 2, act_grad, 0)
-
-    def pool_one(e, _):
-        for half in range(halves):
-            lanes = pl.ds(half * LANES, LANES)
+    lax.fori_loop(0, (prows + 2) // 2, act_grad, 0)
+
+    def pool_one(e):
+        stores = []
+        for half in range(halves):
+            at_half = (e, slice(None), pl.ds(half * LANES, LANES))
             value = stencil(z0, pcoefs, e, e, half).astype(BF16)
-            q1[e, :, lanes] = value
-            z1[e, :, lanes] = value.astype(F32)
-        return 0
-
-    def pool_two(e, _):
-        for half in range(halves):
-            lanes = pl.ds(half * LANES, LANES)
-            q2[e, :, lanes] = (
-                2.0 * stencil(z1, pcoefs, e, e, half) - z0[e, :, lanes]
-            ).astype(BF16)
-        return 0
+            stores += [storing(q1, at_half, value), storing(z1, at_half, value)]
+        return stores
+
+    def pool_two(e):
+        stores = []
+        for half in range(halves):
+            at_half = (e, slice(None), pl.ds(half * LANES, LANES))
+            value = 2.0 * stencil(z1, pcoefs, e, e, half) - z0[at_half]
+            stores += [storing(q2, at_half, value)]
+        return stores
 
     batch = sums.shape[0] // 2
     half_rows = batch // 2
@@ -446,8 +464,8 @@
             sb[pl.ds(t * batch + parts, rest), :] = jnp.zeros((rest, LANES), BF16)
             sums[pl.ds(t * batch + parts, rest), :] = jnp.zeros((rest, LANES), F32)
         for k, term in enumerate(terms):
-            x = term[pl.ds(first, count)].reshape(back.shape[0], feats)
-            value = dot_sum(x, back)
+            x = term[pl.ds(first, count)].reshape(back.shape[1], feats)
+            value = dot(back, x)
             for half in range(halves):
                 place = pl.ds(t * batch + (half * 3 + k) * feats, feats)
                 part = value[:, half * LANES : (half + 1) * LANES]
@@ -510,13 +528,13 @@
             onward.append(send(region, region, peer_a))
         return onward
 
-    back = agm[pl.ds(2, rows)].reshape(rows * width, feats)
-    patch_sums(0, (t0, t1, t2), FINE_UP, rows, back)
+    turned_back[...] = agm[pl.ds(2, rows)].reshape(rows * width, feats).T
+    patch_sums(0, (t0, t1, t2), FINE_UP, rows, turned_back[...])
     fine = start_a(0)
 
-    lax.fori_loop(POOL_UP - 1, prows + POOL_UP + 1, pool_one, 0)
+    by_rows(POOL_UP - 1, prows + POOL_UP + 1, pool_one)
     fine = a_to_b(0, fine)
-    lax.fori_loop(POOL_UP, prows + POOL_UP, pool_two, 0)
+    by_rows(POOL_UP, prows + POOL_UP, pool_two)
     pcol = lax.broadcasted_iota(jnp.int32, (pwidth, feats), 0)
     own_pcols = (pcol >= RIM) & (pcol < pcols + RIM)
 
@@ -526,48 +544,46 @@
 
     lax.fori_loop(0, prows, mask_cot, 0)
 
-    patch_sums(1, (q0, q1, q2), POOL_UP, prows, cm[...].reshape(prows * pwidth, feats))
+    patch_sums(1, (q0, q1, q2), POOL_UP, prows, cm[...].reshape(prows * pwidth, feats).T)
     pool = start_a(1)
 
     top, one, zero = v0, v1, slope
 
     def project_fine(i, _):
-        x = ag[pl.ds(4 * i, 4)].reshape(4 * width, feats)
+        y = dot(ag[pl.ds(4 * i, 4)].reshape(4 * width, feats), w1t[...])
         wide = (4, width, feats)
-        top[pl.ds(4 * i, 4)] = dot_rows(x, w1[2]).astype(BF16).astype(F32).reshape(wide)
-        one[pl.ds(4 * i, 4)] = dot_rows(x, w1[1]).reshape(wide)
-        zero[pl.ds(4 * i, 4)] = dot_rows(x, w1[0]).reshape(wide)
+        top[pl.ds(4 * i, 4)] = y[:, 2 * feats :].astype(BF16).astype(F32).reshape(wide)
+        one[pl.ds(4 * i, 4)] = y[:, feats : 2 * feats].reshape(wide)
+        zero[pl.ds(4 * i, 4)] = y[:, :feats].reshape(wide)
         return 0
 
-    def fine_middle(a, _):
-        for half in range(halves):
-            lanes = pl.ds(half * LANES, LANES)
-            mid[a, :, lanes] = (
-                (one[a, :, lanes] + 2.0 * stencil(top, coefs, a, a + 4, half))
-                .astype(BF16)
-                .astype(F32)
-            )
-        return 0
-
-    def fine_grad(a, _):
-        for half in range(halves):
-            lanes = pl.ds(half * LANES, LANES)
-            value = (
-                zero[a, :, lanes] - top[a, :, lanes] + stencil(mid, coefs, a, a + 4, half)
-            )
-            gp[a - 2, :, lanes] = value[RIM : RIM + cols].astype(BF16)
-        return 0
+    def fine_middle(a):
+        stores = []
+        for half in range(halves):
+            at_half = (a, slice(None), pl.ds(half * LANES, LANES))
+            value = (one[at_half] + 2.0 * stencil(top, coefs, a, a + 4, half)).astype(BF16)
+            stores += [storing(mid, at_half, value)]
+        return stores
+
+    def fine_grad(a):
+        stores = []
+        for half in range(halves):
+            at_half = (a, slice(None), pl.ds(half * LANES, LANES))
+            value = zero[at_half] - top[at_half] + stencil(mid, coefs, a, a + 4, half)
+            out_half = (a - 2, slice(None), at_half[2])
+            stores += [storing(gp, out_half, value[RIM : RIM + cols])]
+        return stores
 
     lax.fori_loop(0, (rows + 4) // 4, project_fine, 0)
     pool = a_to_b(1, pool)
     fine = b_to_c(0, fine)
-    lax.fori_loop(1, rows + 3, fine_middle, 0)
+    by_rows(1, rows + 3, fine_middle)
     fine = c_to_c(0, fine)
     pool = b_to_c(1, pool)
-    lax.fori_loop(2, rows // 2 + 2, fine_grad, 0)
+    by_rows(2, rows // 2 + 2, fine_grad)
     fine = c_to_b(0, fine)
     pool = c_to_c(1, pool)
-    lax.fori_loop(rows // 2 + 2, rows + 2, fine_grad, 0)
+    by_rows(rows // 2 + 2, rows + 2, fine_grad)
     pool = c_to_b(1, pool)
 
     flat = (prows * pwidth, feats)
@@ -589,13 +605,17 @@
                 copy().wait_send()
 
 
-def finish(full, gp, level, gp_out, gfirst, gsecond, level_out):
+def finish(full_in, gp, level, gp_out, gfirst, gsecond, level_out, full, sems):
+    load = pltpu.make_async_copy(full_in, full, sems.at[0])
+    pass_pixels = pltpu.make_async_copy(gp, gp_out, sems.at[1])
+    pass_level = pltpu.make_async_copy(level, level_out, sems.at[2])
+    for copy in (load, pass_pixels, pass_level):
+        copy.start()
+    load.wait()
     feats = gfirst.shape[1]
     halves = feats // LANES
     batch = full.shape[0] // 2
     count = gfirst.shape[0]
-    gp_out[...] = gp[...]
-    level_out[...] = level[...]
     squares = jnp.zeros((8, LANES), F32)
     for t in range(2):
         x = full[pl.ds(t * batch, count * halves), :].astype(F32)
@@ -604,8 +624,11 @@
     factor = jnp.minimum(1.0, 2.0 * feats * lax.rsqrt(square_sum + 1e-06))
     for t, out in enumerate((gfirst, gsecond)):
         for half in range(halves):
-            x = full[pl.ds(t * batch + half * count, count), :].astype(F32)
-            out[:, pl.ds(half * LANES, LANES)] = x * factor
+            for k in range(count // feats):
+                x = full[pl.ds(t * batch + half * count + k * feats, feats), :].astype(F32)
+                out[pl.ds(k * feats + half * LANES, LANES), :] = x.T * factor
+    pass_pixels.wait()
+    pass_level.wait()
 
 
 def shards(groups, members, pixels, offsets, first_weights, second_weights, cotangent):
@@ -647,6 +670,7 @@
     scratch += [vm((phigh, pwidth, feats), BF16), vm((prows, pwidth, feats), BF16)]
     scratch += [vm((phigh, pwidth, feats), t) for t in (BF16,) * 3 + (F32,) * 7]
     scratch += [vm((bhigh, width, feats), t) for t in (BF16, BF16, F32)]
+    scratch += [vm((feats, 3 * feats), BF16)] * 2 + [vm((feats, rows * width), BF16)]
     scratch += [
         vm((2 * total, LANES), F32), vm((2 * total, LANES), BF16),
         vm((2, half, LANES), BF16),
@@ -656,6 +680,7 @@
     scratch += [pltpu.SemaphoreType.DMA((3, orders))] * 2
     copies = 2 * (3 * groups + 2 * lines - 3)
     scratch += [pltpu.SemaphoreType.DMA((copies,))] * 2
+    held, anywhere = pl.BlockSpec(memory_space=pltpu.VMEM), pl.BlockSpec(memory_space=pl.ANY)
     inner_pixels, full, inner_level = pl.pallas_call(
         functools.partial(kernel, groups, members, chunk),
         out_shape=(
@@ -663,8 +688,8 @@
             jax.ShapeDtypeStruct((2 * total, LANES), BF16),
             jax.ShapeDtypeStruct(cotangent.shape, BF16),
         ),
-        in_specs=[pl.BlockSpec(memory_space=pltpu.VMEM)] * 5,
-        out_specs=[pl.BlockSpec(memory_space=pltpu.VMEM)] * 3,
+        in_specs=[held] * 5,
+        out_specs=[held] * 3,
         scratch_shapes=scratch,
         compiler_params=pltpu.CompilerParams(
             collective_id=0, has_side_effects=True, vmem_limit_bytes=60 * 1024 * 1024
@@ -678,9 +703,10 @@
             jax.ShapeDtypeStruct((3 * feats, feats), F32),
             jax.ShapeDtypeStruct(cotangent.shape, BF16),
         ),
-        in_specs=[pl.BlockSpec(memory_space=pltpu.VMEM)] * 3,
-        out_specs=[pl.BlockSpec(memory_space=pltpu.VMEM)] * 4,
-        compiler_params=pltpu.CompilerParams(vmem_limit_bytes=40 * 1024 * 1024),
+        in_specs=[anywhere] * 3,
+        out_specs=[anywhere, held, held, anywhere],
+        scratch_shapes=[vm((2 * total, LANES), BF16), pltpu.SemaphoreType.DMA((3,))],
+        compiler_params=pltpu.CompilerParams(vmem_limit_bytes=60 * 1024 * 1024),
     )(full, inner_pixels, inner_level)
     shape = first_weights.shape
     return grad_pixels, first.reshape(shape), second.reshape(shape), level

time: 59.2 us -> 75 us (1.27)
  Pallas kernels: 55.2 us -> 74.2 us
  local copies, waits for them, and re-layouts: 3.07 us -> 0 us
    pallas_call x1, Pallas kernels: 1.56 us -> 22.1 us  [shards(): pl.pallas_call(finish, out_shape=(jax.ShapeDtypeStruct(pixels.shape, BF16...]
    unnamed x6 -> x0, local copies, waits for them, and re-layouts: 3.07 us -> none
    pallas_call x1, Pallas kernels: 53.7 us -> 52 us  [shards(): pl.pallas_call(functools.partial(kernel, groups, members, chunk), out_sha...]
where the time goes in v3:
time: 75 us; the launch traced here: 74.8 us
  Pallas kernels  74.2 us (99%)
    pallas_call x1, Pallas kernels, shards(): pl.pallas_call(functools.partial(kernel, groups, members, chunk), out_sha...  52 us
    pallas_call x1, Pallas kernels, shards(): pl.pallas_call(finish, out_shape=(jax.ShapeDtypeStruct(pixels.shape, BF16...  22.1 us

profile of v3, /device:TPU:0, one launch (start us, length us, event | category | flops | bytes accessed | tf_op | source)
XLA Modules:
  0.0 74.8 jit_solution(6183720315618645026)
XLA Ops:
  0.6 52.0 %shard_map.84 = (bf16[16,64,256]{2,1,0:T(8,128)(2,1)}, bf16[3072,128]{1,0:T(8,128)(2,1)}, bf16[8,32,256]{2,1,0:T(8,128)(2,1)}) custom-call(bf16[16,64,256]{2,1,0:T(8,128)(2,1)} %px.1, f32[16,64]{1,0:T(8,128)} %off.1, bf16[3,256,256]{2,1,0:T(8,128)(2,1)} %w1.1, bf16[3,256,256]{2,1,0:T(8,128)(2,1)} %w2.1, bf16[8,32,256]{2,1,0:T(8,128)(2,1)} %cot.1), custom_call_target="tpu_custom_call" | custom-call | tf_op jit(solution)/shard_map/pallas_call | solution.py:684
  52.7 22.1 %shard_map.85 = (bf16[16,64,256]{2,1,0:T(8,128)(2,1)}, f32[768,256]{1,0:T(8,128)}, f32[768,256]{1,0:T(8,128)}, bf16[8,32,256]{2,1,0:T(8,128)(2,1)}) custom-call(bf16[3072,128]{1,0:T(8,128)(2,1)} %get-tuple-element.11.full_in, bf16[16,64,256]{2,1,0:T(8,128)(2,1)} %get-tuple-element.12.gp, bf16[8,32,256]{2,1,0:T(8,128)(2,1)} %get-tuple-element.13.level), custom_call_target="tpu_custom_call" | custom-call | tf_op jit(solution)/shard_map/pallas_call | solution.py:698

commit v4 on v3

--- a/solution.py
+++ b/solution.py
@@ -370,8 +370,8 @@
             stores += [storing(t2, at_half, value)]
         return stores
 
-    by_rows(1, rows + 2 * FINE_UP - 1, fine_one)
-    by_rows(2, rows + 2 * FINE_UP - 2, fine_two)
+    by_rows(FINE_UP - 1, rows + FINE_UP + 1, fine_one)
+    by_rows(FINE_UP, rows + FINE_UP, fine_two)
 
     def pool_matrix(shape, fine_dim, repeat):
         f = lax.broadcasted_iota(jnp.int32, shape, fine_dim)
@@ -403,20 +403,25 @@
             z0[2 + 2 * i + p] = part.astype(F32)
         return 0
 
-    lax.fori_loop(0, (prows + 4) // 2, activate, 0)
+    lax.fori_loop(1, prows // 2 + 1, activate, 0)
 
     col = lax.broadcasted_iota(jnp.int32, (width, feats), 0)
     own_cols = (col >= RIM) & (col < cols + RIM)
 
+    def act_pair(blocks, masked):
+        wide = split_dot(spread_pool, [pgrad[POOL_UP + p] for p in blocks])
+        for b, p in enumerate(blocks):
+            for r in (0, 1):
+                value = wide[:, b * feats : (b + 1) * feats] * slope[2 * p + 4 + r]
+                ag[2 * p + 2 + r] = value.astype(BF16)
+                if masked:
+                    agm[2 * p + r] = jnp.where(own_cols, value, 0.0).astype(BF16)
+
     def act_grad(i, _):
-        wide = split_dot(spread_pool, [pgrad[3 + 2 * i], pgrad[4 + 2 * i]])
-        for r in range(4):
-            value = wide[:, (r // 2) * feats : (r // 2 + 1) * feats] * slope[4 * i + 2 + r]
-            ag[4 * i + r] = value.astype(BF16)
-            agm[4 * i + r] = jnp.where(own_cols, value, 0.0).astype(BF16)
+        act_pair((2 * i, 2 * i + 1), True)
         return 0
 
-    lax.fori_loop(0, (prows + 2) // 2, act_grad, 0)
+    lax.fori_loop(0, prows // 2, act_grad, 0)
 
     def pool_one(e):
         stores = []
@@ -528,13 +533,21 @@
             onward.append(send(region, region, peer_a))
         return onward
 
-    turned_back[...] = agm[pl.ds(2, rows)].reshape(rows * width, feats).T
+    turned_back[...] = agm[...].reshape(rows * width, feats).T
     patch_sums(0, (t0, t1, t2), FINE_UP, rows, turned_back[...])
     fine = start_a(0)
 
+    by_rows(1, FINE_UP - 1, fine_one)
+    by_rows(rows + FINE_UP + 1, rows + 2 * FINE_UP - 1, fine_one)
+    by_rows(2, FINE_UP, fine_two)
+    by_rows(rows + FINE_UP, rows + 2 * FINE_UP - 2, fine_two)
+    fine = a_to_b(0, fine)
+    lax.fori_loop(0, 2, lambda j, c: activate(j * (prows // 2 + 1), c), 0)
+    act_pair((-1, prows), False)
     by_rows(POOL_UP - 1, prows + POOL_UP + 1, pool_one)
-    fine = a_to_b(0, fine)
     by_rows(POOL_UP, prows + POOL_UP, pool_two)
+    fine = b_to_c(0, fine)
+
     pcol = lax.broadcasted_iota(jnp.int32, (pwidth, feats), 0)
     own_pcols = (pcol >= RIM) & (pcol < pcols + RIM)
 
@@ -575,15 +588,15 @@
         return stores
 
     lax.fori_loop(0, (rows + 4) // 4, project_fine, 0)
+    fine = c_to_c(0, fine)
     pool = a_to_b(1, pool)
-    fine = b_to_c(0, fine)
     by_rows(1, rows + 3, fine_middle)
-    fine = c_to_c(0, fine)
+    fine = c_to_b(0, fine)
     pool = b_to_c(1, pool)
     by_rows(2, rows // 2 + 2, fine_grad)
-    fine = c_to_b(0, fine)
     pool = c_to_c(1, pool)
     by_rows(rows // 2 + 2, rows + 2, fine_grad)
+    fine = b_to_a(0, fine)
     pool = c_to_b(1, pool)
 
     flat = (prows * pwidth, feats)
@@ -594,7 +607,6 @@
         start = r * pwidth + RIM
         level[r] = out[start : start + pcols].astype(BF16)
 
-    fine = b_to_a(0, fine)
     pool = b_to_a(1, pool)
     for copy in fine + pool:
         copy.wait()
@@ -605,12 +617,20 @@
                 copy().wait_send()
 
 
-def finish(full_in, gp, level, gp_out, gfirst, gsecond, level_out, full, sems):
+def finish(
+    full_in, gp, level, gp_out, gfirst, gsecond, level_out, full, gp_held, level_held, sems
+):
     load = pltpu.make_async_copy(full_in, full, sems.at[0])
-    pass_pixels = pltpu.make_async_copy(gp, gp_out, sems.at[1])
-    pass_level = pltpu.make_async_copy(level, level_out, sems.at[2])
-    for copy in (load, pass_pixels, pass_level):
+    load_pixels = pltpu.make_async_copy(gp, gp_held, sems.at[1])
+    load_level = pltpu.make_async_copy(level, level_held, sems.at[2])
+    pass_pixels = pltpu.make_async_copy(gp_held, gp_out, sems.at[3])
+    pass_level = pltpu.make_async_copy(level_held, level_out, sems.at[4])
+    for copy in (load, load_pixels, load_level):
         copy.start()
+    load_pixels.wait()
+    pass_pixels.start()
+    load_level.wait()
+    pass_level.start()
     load.wait()
     feats = gfirst.shape[1]
     halves = feats // LANES
@@ -669,7 +689,7 @@
     scratch += [vm((rows + 8, width, feats), F32)]
     scratch += [vm((phigh, pwidth, feats), BF16), vm((prows, pwidth, feats), BF16)]
     scratch += [vm((phigh, pwidth, feats), t) for t in (BF16,) * 3 + (F32,) * 7]
-    scratch += [vm((bhigh, width, feats), t) for t in (BF16, BF16, F32)]
+    scratch += [vm((n, width, feats), t) for n, t in ((bhigh, BF16), (rows, BF16), (bhigh, F32))]
     scratch += [vm((feats, 3 * feats), BF16)] * 2 + [vm((feats, rows * width), BF16)]
     scratch += [
         vm((2 * total, LANES), F32), vm((2 * total, LANES), BF16),
@@ -705,7 +725,10 @@
         ),
         in_specs=[anywhere] * 3,
         out_specs=[anywhere, held, held, anywhere],
-        scratch_shapes=[vm((2 * total, LANES), BF16), pltpu.SemaphoreType.DMA((3,))],
+        scratch_shapes=[
+            vm((2 * total, LANES), BF16), vm(pixels.shape, BF16), vm(cotangent.shape, BF16),
+            pltpu.SemaphoreType.DMA((5,)),
+        ],
         compiler_params=pltpu.CompilerParams(vmem_limit_bytes=60 * 1024 * 1024),
     )(full, inner_pixels, inner_level)
     shape = first_weights.shape

time: 75 us -> 57.5 us (0.77)
  Pallas kernels: 74.2 us -> 56.7 us
    pallas_call x1, Pallas kernels: 22.1 us -> 3.29 us  [shards(): pl.pallas_call(finish, out_shape=(jax.ShapeDtypeStruct(pixels.shape, BF16...]
    pallas_call x1, Pallas kernels: 52 us -> 53.4 us  [shards(): pl.pallas_call(functools.partial(kernel, groups, members, chunk), out_sha...]
where the time goes in v4:
time: 57.5 us; the launch traced here: 57.3 us
  Pallas kernels  56.7 us (99%)
  between operations  0.64 us (1%)
    pallas_call x1, Pallas kernels, shards(): pl.pallas_call(functools.partial(kernel, groups, members, chunk), out_sha...  53.4 us
    pallas_call x1, Pallas kernels, shards(): pl.pallas_call(finish, out_shape=(jax.ShapeDtypeStruct(pixels.shape, BF16...  3.29 us

profile of v4, /device:TPU:0, one launch (start us, length us, event | category | flops | bytes accessed | tf_op | source)
XLA Modules:
  0.0 57.3 jit_solution(18088276922413491099)
XLA Ops:
  0.6 53.4 %shard_map.84 = (bf16[16,64,256]{2,1,0:T(8,128)(2,1)}, bf16[3072,128]{1,0:T(8,128)(2,1)}, bf16[8,32,256]{2,1,0:T(8,128)(2,1)}) custom-call(bf16[16,64,256]{2,1,0:T(8,128)(2,1)} %px.1, f32[16,64]{1,0:T(8,128)} %off.1, bf16[3,256,256]{2,1,0:T(8,128)(2,1)} %w1.1, bf16[3,256,256]{2,1,0:T(8,128)(2,1)} %w2.1, bf16[8,32,256]{2,1,0:T(8,128)(2,1)} %cot.1), custom_call_target="tpu_custom_call" | custom-call | tf_op jit(solution)/shard_map/pallas_call | solution.py:704
  54.1 3.3 %shard_map.85 = (bf16[16,64,256]{2,1,0:T(8,128)(2,1)}, f32[768,256]{1,0:T(8,128)}, f32[768,256]{1,0:T(8,128)}, bf16[8,32,256]{2,1,0:T(8,128)(2,1)}) custom-call(bf16[3072,128]{1,0:T(8,128)(2,1)} %get-tuple-element.11.full_in, bf16[16,64,256]{2,1,0:T(8,128)(2,1)} %get-tuple-element.12.gp, bf16[8,32,256]{2,1,0:T(8,128)(2,1)} %get-tuple-element.13.level), custom_call_target="tpu_custom_call" | custom-call | tf_op jit(solution)/shard_map/pallas_call | solution.py:718

commit v5 on v3

--- a/solution.py
+++ b/solution.py
@@ -61,7 +61,9 @@
     for b in range(stack.shape[0] // LANES):
         turned[b] = stack[pl.ds(b * LANES, LANES), :].T
     width = coefs.shape[2]
-    for k in range(len(STEPS)):
+    for k, step in enumerate(STEPS):
+        if step[:2] == (1, 0):
+            continue
         for e in range(first, last):
             block, lane = divmod(k * rows + e + shift, LANES)
             coefs[k, e] = jnp.broadcast_to(
@@ -69,40 +71,57 @@
             )
 
 
-def stencil(values, coefs, row, coef_row, half):
-    lanes = pl.ds(half * LANES, LANES)
-    around = [values[row + dr, :, lanes] for dr in (-1, 0, 1)]
-    width = around[0].shape[0]
-
-    def column(dc):
-        total = None
-        for dr in (-1, 0, 1):
-            if (dr, dc) in INDEX:
-                term = coefs[INDEX[dr, dc], coef_row] * around[dr + 1]
-                total = term if total is None else total + term
-        return total
-
-    return pltpu.roll(column(-1), 1, 0) + column(0) + pltpu.roll(column(1), width - 1, 0)
+def stencil(values, coefs, row, coef_row, emit, lead=0):
+    tiles = values.shape[1] // 8
+    halves = values.shape[2] // LANES
+    line = lax.broadcasted_iota(jnp.int32, (8, LANES), 0)
+    first, last = line == 0, line == 7
+    before = [None] * halves
+    done = [[] for _ in range(halves)]
+
+    def close(half, left, centre, right, after):
+        done[half].append(left + centre + jnp.where(last, after, right))
+        j = len(done[half]) - 1
+        if j > lead and (j - lead) % 2:
+            emit(8 * (j - 1), half, jnp.concatenate(done[half][-2:], axis=0))
+
+    for j in range(tiles):
+        cols = pl.ds(8 * j, 8)
+        weight = {
+            (dr, dc): coefs[k, coef_row, cols]
+            for (dr, dc), k in INDEX.items()
+            if (dr, dc) != (1, 0)
+        }
+        weight[1, 0] = coefs[INDEX[-1, 0], coef_row + 1, cols]
+        for half in range(halves):
+            up, centre, down = (
+                values[row + dr, cols, pl.ds(half * LANES, LANES)] for dr in (-1, 0, 1)
+            )
+            to_right = weight[-1, -1] * up + weight[0, -1] * centre + weight[1, -1] * down
+            to_left = weight[-1, 1] * up + weight[0, 1] * centre + weight[1, 1] * down
+            straight = weight[-1, 0] * up + weight[1, 0] * down
+            to_right = pltpu.roll(to_right, 1, 0)
+            to_left = pltpu.roll(to_left, 7, 0)
+            left = to_right
+            if j:
+                old_right, old_left, old_straight, old_to_left = before[half]
+                left = jnp.where(first, old_right, to_right)
+                close(half, old_left, old_straight, old_to_left, to_left)
+            before[half] = (to_right, left, straight, to_left)
+    for half in range(halves):
+        _, left, straight, to_left = before[half]
+        close(half, left, straight, to_left, to_left)
 
 
 def by_rows(first, last, work):
     def two(i, _):
-        e = first + 2 * i
-        for store in work(e) + work(e + 1):
-            store()
+        work(first + 2 * i)
+        work(first + 2 * i + 1)
         return 0
 
     lax.fori_loop(0, (last - first) // 2, two, 0)
     if (last - first) % 2:
-        for store in work(last - 1):
-            store()
-
-
-def storing(ref, index, value):
-    def store():
-        ref[index] = value.astype(ref.dtype)
-
-    return store
+        work(last - 1)
 
 
 def dot(a, b):
@@ -283,7 +302,7 @@
     )
     spread_coefficients(
         edge_coefficients(poffsets, pinside), pstack, pturned, pcoefs, 0, 1,
-        prows + 2 * POOL_UP - 1,
+        prows + 2 * POOL_UP,
     )
 
     def assemble(store, start, pairs, middle, left, right):
@@ -330,45 +349,43 @@
     lax.fori_loop(0, (prows + 2 * POOL_UP) // 4, project_pool, 0)
 
     def pool_middle(e):
-        stores = []
-        for half in range(halves):
-            at_half = (e, slice(None), pl.ds(half * LANES, LANES))
-            value = (pone[at_half] + 2.0 * stencil(ptop, pcoefs, e, e, half)).astype(BF16)
-            stores += [storing(pmid, at_half, value)]
-        return stores
+        def emit(col, half, value):
+            at = (e, pl.ds(col, 16), pl.ds(half * LANES, LANES))
+            pmid[at] = (pone[at] + 2.0 * value).astype(BF16).astype(F32)
+
+        stencil(ptop, pcoefs, e, e, emit)
 
     def pool_grad(e):
-        stores = []
-        for half in range(halves):
-            at_half = (e, slice(None), pl.ds(half * LANES, LANES))
-            value = pzero[at_half] - ptop[at_half] + stencil(pmid, pcoefs, e, e, half)
-            stores += [storing(pgrad, at_half, value)]
-        return stores
+        def emit(col, half, value):
+            at = (e, pl.ds(col, 16), pl.ds(half * LANES, LANES))
+            pgrad[at] = pzero[at] - ptop[at] + value
+
+        stencil(pmid, pcoefs, e, e, emit)
 
     by_rows(2, prows + 2 * POOL_UP - 2, pool_middle)
     by_rows(3, prows + 2 * POOL_UP - 3, pool_grad)
 
     spread_coefficients(
-        edge_coefficients(offsets, inside), stack, turned, coefs, 2, 1, rows + 2 * FINE_UP - 1
+        edge_coefficients(offsets, inside), stack, turned, coefs, 2, 1, rows + 2 * FINE_UP
     )
     receive(0)
     assemble_all(store_px, px, FINE_UP, px_v, px_h, px_c)
 
     def fine_one(e):
-        stores = []
-        for half in range(halves):
-            at_half = (e, slice(None), pl.ds(half * LANES, LANES))
-            value = stencil(v0, coefs, e, e, half).astype(BF16)
-            stores += [storing(t1, at_half, value), storing(v1, at_half, value)]
-        return stores
+        def emit(col, half, value):
+            at = (e, pl.ds(col, 16), pl.ds(half * LANES, LANES))
+            value = value.astype(BF16)
+            t1[at] = value
+            v1[at] = value.astype(F32)
+
+        stencil(v0, coefs, e, e, emit)
 
     def fine_two(e):
-        stores = []
-        for half in range(halves):
-            at_half = (e, slice(None), pl.ds(half * LANES, LANES))
-            value = 2.0 * stencil(v1, coefs, e, e, half) - v0[at_half]
-            stores += [storing(t2, at_half, value)]
-        return stores
+        def emit(col, half, value):
+            at = (e, pl.ds(col, 16), pl.ds(half * LANES, LANES))
+            t2[at] = (2.0 * value - v0[at]).astype(BF16)
+
+        stencil(v1, coefs, e, e, emit)
 
     by_rows(1, rows + 2 * FINE_UP - 1, fine_one)
     by_rows(2, rows + 2 * FINE_UP - 2, fine_two)
@@ -419,20 +436,20 @@
     lax.fori_loop(0, (prows + 2) // 2, act_grad, 0)
 
     def pool_one(e):
-        stores = []
-        for half in range(halves):
-            at_half = (e, slice(None), pl.ds(half * LANES, LANES))
-            value = stencil(z0, pcoefs, e, e, half).astype(BF16)
-            stores += [storing(q1, at_half, value), storing(z1, at_half, value)]
-        return stores
+        def emit(col, half, value):
+            at = (e, pl.ds(col, 16), pl.ds(half * LANES, LANES))
+            value = value.astype(BF16)
+            q1[at] = value
+            z1[at] = value.astype(F32)
+
+        stencil(z0, pcoefs, e, e, emit)
 
     def pool_two(e):
-        stores = []
-        for half in range(halves):
-            at_half = (e, slice(None), pl.ds(half * LANES, LANES))
-            value = 2.0 * stencil(z1, pcoefs, e, e, half) - z0[at_half]
-            stores += [storing(q2, at_half, value)]
-        return stores
+        def emit(col, half, value):
+            at = (e, pl.ds(col, 16), pl.ds(half * LANES, LANES))
+            q2[at] = (2.0 * value - z0[at]).astype(BF16)
+
+        stencil(z1, pcoefs, e, e, emit)
 
     batch = sums.shape[0] // 2
     half_rows = batch // 2
@@ -558,21 +575,20 @@
         return 0
 
     def fine_middle(a):
-        stores = []
-        for half in range(halves):
-            at_half = (a, slice(None), pl.ds(half * LANES, LANES))
-            value = (one[at_half] + 2.0 * stencil(top, coefs, a, a + 4, half)).astype(BF16)
-            stores += [storing(mid, at_half, value)]
-        return stores
+        def emit(col, half, value):
+            at = (a, pl.ds(col, 16), pl.ds(half * LANES, LANES))
+            mid[at] = (one[at] + 2.0 * value).astype(BF16).astype(F32)
+
+        stencil(top, coefs, a, a + 4, emit)
 
     def fine_grad(a):
-        stores = []
-        for half in range(halves):
-            at_half = (a, slice(None), pl.ds(half * LANES, LANES))
-            value = zero[at_half] - top[at_half] + stencil(mid, coefs, a, a + 4, half)
-            out_half = (a - 2, slice(None), at_half[2])
-            stores += [storing(gp, out_half, value[RIM : RIM + cols])]
-        return stores
+        def emit(col, half, value):
+            at = (a, pl.ds(col, 16), pl.ds(half * LANES, LANES))
+            if col + 16 <= RIM + cols:
+                out = (a - 2, pl.ds(col - RIM, 16), at[2])
+                gp[out] = (zero[at] - top[at] + value).astype(BF16)
+
+        stencil(mid, coefs, a, a + 4, emit, lead=1)
 
     lax.fori_loop(0, (rows + 4) // 4, project_fine, 0)
     pool = a_to_b(1, pool)
@@ -605,12 +621,20 @@
                 copy().wait_send()
 
 
-def finish(full_in, gp, level, gp_out, gfirst, gsecond, level_out, full, sems):
+def finish(
+    full_in, gp, level, gp_out, gfirst, gsecond, level_out, full, gp_held, level_held, sems
+):
     load = pltpu.make_async_copy(full_in, full, sems.at[0])
-    pass_pixels = pltpu.make_async_copy(gp, gp_out, sems.at[1])
-    pass_level = pltpu.make_async_copy(level, level_out, sems.at[2])
-    for copy in (load, pass_pixels, pass_level):
+    load_pixels = pltpu.make_async_copy(gp, gp_held, sems.at[1])
+    load_level = pltpu.make_async_copy(level, level_held, sems.at[2])
+    pass_pixels = pltpu.make_async_copy(gp_held, gp_out, sems.at[3])
+    pass_level = pltpu.make_async_copy(level_held, level_out, sems.at[4])
+    for copy in (load, load_pixels, load_level):
         copy.start()
+    load_pixels.wait()
+    pass_pixels.start()
+    load_level.wait()
+    pass_level.start()
     load.wait()
     feats = gfirst.shape[1]
     halves = feats // LANES
@@ -705,7 +729,10 @@
         ),
         in_specs=[anywhere] * 3,
         out_specs=[anywhere, held, held, anywhere],
-        scratch_shapes=[vm((2 * total, LANES), BF16), pltpu.SemaphoreType.DMA((3,))],
+        scratch_shapes=[
+            vm((2 * total, LANES), BF16), vm(pixels.shape, BF16), vm(cotangent.shape, BF16),
+            pltpu.SemaphoreType.DMA((5,)),
+        ],
         compiler_params=pltpu.CompilerParams(vmem_limit_bytes=60 * 1024 * 1024),
     )(full, inner_pixels, inner_level)
     shape = first_weights.shape

time: 75 us -> 55.9 us (0.75)
  Pallas kernels: 74.2 us -> 55.1 us
    pallas_call x1, Pallas kernels: 22.1 us -> 3.29 us  [shards(): pl.pallas_call(finish, out_shape=(jax.ShapeDtypeStruct(pixels.shape, BF16...]
where the time goes in v5:
time: 55.9 us; the launch traced here: 55.7 us
  Pallas kernels  55.1 us (99%)
  between operations  0.64 us (1%)
    pallas_call x1, Pallas kernels, shards(): pl.pallas_call(functools.partial(kernel, groups, members, chunk), out_sha...  51.8 us
    pallas_call x1, Pallas kernels, shards(): pl.pallas_call(finish, out_shape=(jax.ShapeDtypeStruct(pixels.shape, BF16...  3.29 us

profile of v5, /device:TPU:0, one launch (start us, length us, event | category | flops | bytes accessed | tf_op | source)
XLA Modules:
  0.0 55.7 jit_solution(17529643196823193512)
XLA Ops:
  0.6 51.8 %shard_map.84 = (bf16[16,64,256]{2,1,0:T(8,128)(2,1)}, bf16[3072,128]{1,0:T(8,128)(2,1)}, bf16[8,32,256]{2,1,0:T(8,128)(2,1)}) custom-call(bf16[16,64,256]{2,1,0:T(8,128)(2,1)} %px.1, f32[16,64]{1,0:T(8,128)} %off.1, bf16[3,256,256]{2,1,0:T(8,128)(2,1)} %w1.1, bf16[3,256,256]{2,1,0:T(8,128)(2,1)} %w2.1, bf16[8,32,256]{2,1,0:T(8,128)(2,1)} %cot.1), custom_call_target="tpu_custom_call" | custom-call | tf_op jit(solution)/shard_map/pallas_call | solution.py:708
  52.4 3.3 %shard_map.85 = (bf16[16,64,256]{2,1,0:T(8,128)(2,1)}, f32[768,256]{1,0:T(8,128)}, f32[768,256]{1,0:T(8,128)}, bf16[8,32,256]{2,1,0:T(8,128)(2,1)}) custom-call(bf16[3072,128]{1,0:T(8,128)(2,1)} %get-tuple-element.11.full_in, bf16[16,64,256]{2,1,0:T(8,128)(2,1)} %get-tuple-element.12.gp, bf16[8,32,256]{2,1,0:T(8,128)(2,1)} %get-tuple-element.13.level), custom_call_target="tpu_custom_call" | custom-call | tf_op jit(solution)/shard_map/pallas_call | solution.py:722

commit v6 on v5

--- a/solution.py
+++ b/solution.py
@@ -137,7 +137,7 @@
 
 def kernel(
     groups, members, chunk,
-    px, off, w1, w2, cot,
+    px, off, w1_in, w2_in, cot,
     gp, full, level,
     off_own, off_in,
     px_pack, px_v, px_h, px_c,
@@ -145,7 +145,7 @@
     off_ext, stack, turned, pstack, pturned, coefs, pcoefs,
     t0, t1, t2, v0, v1, slope,
     c0, cm, q0, q1, q2, z0, z1, ptop, pone, pzero, pmid, pgrad,
-    ag, agm, mid, w1t, w2t, turned_back,
+    ag, agm, mid, w1t, w2t, turned_back, w1, w2, weight_sems,
     sums, sb, in_a, in_b, in_c,
     halo_send, halo_recv, sum_send, sum_recv,
 ):
@@ -170,6 +170,13 @@
     for j in range(1, lines):
         z = lax.rem(line + j, lines)
         peers_c.append((z, (g, z * 2 + lax.rem(d, 2))))
+
+    fetches = [
+        pltpu.make_async_copy(w2_in, w2, weight_sems.at[0]),
+        pltpu.make_async_copy(w1_in, w1, weight_sems.at[1]),
+    ]
+    for copy in fetches:
+        copy.start()
 
     barrier = pltpu.get_barrier_semaphore()
     for dr, dc, exists, peer in around:
@@ -254,7 +261,8 @@
             def _():
                 halo_copies(dr, dc, peer)[1][a][1]().wait_recv()
 
-    for source, target in ((w2, w2t), (w1, w1t)):
+    for copy, source, target in zip(fetches, (w2, w1), (w2t, w1t)):
+        copy.wait()
         for k in range(source.shape[0]):
             target[:, pl.ds(k * feats, feats)] = source[k].T
     receive(2)
@@ -622,7 +630,8 @@
 
 
 def finish(
-    full_in, gp, level, gp_out, gfirst, gsecond, level_out, full, gp_held, level_held, sems
+    full_in, gp, level, gp_out, gfirst, gsecond, level_out, full, gp_held, level_held,
+    scaled, sems, out_sems,
 ):
     load = pltpu.make_async_copy(full_in, full, sems.at[0])
     load_pixels = pltpu.make_async_copy(gp, gp_held, sems.at[1])
@@ -646,11 +655,19 @@
         squares = squares + jnp.sum((x * x).reshape(count * halves // 8, 8, LANES), axis=0)
     square_sum = jnp.sum(jnp.sum(squares, axis=0, keepdims=True), axis=1, keepdims=True)
     factor = jnp.minimum(1.0, 2.0 * feats * lax.rsqrt(square_sum + 1e-06))
+    sent = []
     for t, out in enumerate((gfirst, gsecond)):
-        for half in range(halves):
-            for k in range(count // feats):
+        for k in range(count // feats):
+            place = pl.ds(k * feats, feats)
+            for half in range(halves):
                 x = full[pl.ds(t * batch + half * count + k * feats, feats), :].astype(F32)
-                out[pl.ds(k * feats + half * LANES, LANES), :] = x.T * factor
+                scaled[t, pl.ds(k * feats + half * LANES, LANES), :] = x.T * factor
+            sent.append(
+                pltpu.make_async_copy(scaled.at[t, place], out.at[place], out_sems.at[t, k])
+            )
+            sent[-1].start()
+    for copy in sent:
+        copy.wait()
     pass_pixels.wait()
     pass_level.wait()
 
@@ -695,6 +712,7 @@
     scratch += [vm((phigh, pwidth, feats), t) for t in (BF16,) * 3 + (F32,) * 7]
     scratch += [vm((bhigh, width, feats), t) for t in (BF16, BF16, F32)]
     scratch += [vm((feats, 3 * feats), BF16)] * 2 + [vm((feats, rows * width), BF16)]
+    scratch += [vm(first_weights.shape, BF16)] * 2 + [pltpu.SemaphoreType.DMA((2,))]
     scratch += [
         vm((2 * total, LANES), F32), vm((2 * total, LANES), BF16),
         vm((2, half, LANES), BF16),
@@ -712,7 +730,7 @@
             jax.ShapeDtypeStruct((2 * total, LANES), BF16),
             jax.ShapeDtypeStruct(cotangent.shape, BF16),
         ),
-        in_specs=[held] * 5,
+        in_specs=[held, held, anywhere, anywhere, held],
         out_specs=[held] * 3,
         scratch_shapes=scratch,
         compiler_params=pltpu.CompilerParams(
@@ -728,10 +746,11 @@
             jax.ShapeDtypeStruct(cotangent.shape, BF16),
         ),
         in_specs=[anywhere] * 3,
-        out_specs=[anywhere, held, held, anywhere],
+        out_specs=[anywhere] * 4,
         scratch_shapes=[
             vm((2 * total, LANES), BF16), vm(pixels.shape, BF16), vm(cotangent.shape, BF16),
-            pltpu.SemaphoreType.DMA((5,)),
+            vm((2, 3 * feats, feats), F32),
+            pltpu.SemaphoreType.DMA((5,)), pltpu.SemaphoreType.DMA((2, 3)),
         ],
         compiler_params=pltpu.CompilerParams(vmem_limit_bytes=60 * 1024 * 1024),
     )(full, inner_pixels, inner_level)

time: 55.9 us -> 55.4 us (level)
  no operation moved by 1% of the time
where the time goes in v6:
time: 55.4 us; the launch traced here: 55.2 us
  Pallas kernels  54.6 us (99%)
  between operations  0.64 us (1%)
    pallas_call x1, Pallas kernels, shards(): pl.pallas_call(functools.partial(kernel, groups, members, chunk), out_sha...  51.6 us
    pallas_call x1, Pallas kernels, shards(): pl.pallas_call(finish, out_shape=(jax.ShapeDtypeStruct(pixels.shape, BF16...  3.04 us

profile of v6, /device:TPU:0, one launch (start us, length us, event | category | flops | bytes accessed | tf_op | source)
XLA Modules:
  0.0 55.2 jit_solution(7684957239535486885)
XLA Ops:
  0.6 51.6 %shard_map.84 = (bf16[16,64,256]{2,1,0:T(8,128)(2,1)}, bf16[3072,128]{1,0:T(8,128)(2,1)}, bf16[8,32,256]{2,1,0:T(8,128)(2,1)}) custom-call(bf16[16,64,256]{2,1,0:T(8,128)(2,1)} %px.1, f32[16,64]{1,0:T(8,128)} %off.1, bf16[3,256,256]{2,1,0:T(8,128)(2,1)} %w1_in.1, bf16[3,256,256]{2,1,0:T(8,128)(2,1)} %w2_in.1, bf16[8,32,256]{2,1,0:T(8,128)(2,1)} %cot.1), custom_call_target="tpu_custom_call" | custom-call | tf_op jit(solution)/shard_map/pallas_call | solution.py:726
  52.2 3.0 %shard_map.85 = (bf16[16,64,256]{2,1,0:T(8,128)(2,1)}, f32[768,256]{1,0:T(8,128)}, f32[768,256]{1,0:T(8,128)}, bf16[8,32,256]{2,1,0:T(8,128)(2,1)}) custom-call(bf16[3072,128]{1,0:T(8,128)(2,1)} %get-tuple-element.11.full_in, bf16[16,64,256]{2,1,0:T(8,128)(2,1)} %get-tuple-element.12.gp, bf16[8,32,256]{2,1,0:T(8,128)(2,1)} %get-tuple-element.13.level), custom_call_target="tpu_custom_call" | custom-call | tf_op jit(solution)/shard_map/pallas_call | solution.py:740
